TPU v7x, 512 devices: a whole 4x4x16 slice. The times are simulated.
512 devices in a mesh: ctx: 64 (over z_lo, y, core), section: 8 (over x, z_hi).
Axes of the slice: x: 4, y: 4, z: 16 (z_hi: 2, z_lo: 8; z = z_hi * 8 + z_lo), core: 2. Of those that a mesh axis runs over, the one named last changes fastest.
Arguments:
- gate: bfloat16 [8, 8192, 4096], P('section', 'ctx'), may hold values from -6 to 6
- grad_out: bfloat16 [8, 8192, 4096], P('section', 'ctx'), may hold values from -6 to 6
- decay: float32 [8, 16, 4096], P('section'), may hold values from 3.0517578e-05 to 0.0333333333, as said below
- amplitude: float32 [8, 16, 4096], P('section'), may hold values from -0.2581989 to 0.2581989, as said below
Outputs:
- passed: bfloat16 [8, 8192, 4096], P('section', 'ctx')
Inputs may be any that keep to these rules, and one draw needn't show every extreme that they name: `decay`: decay rates per position of the filter's modes. `amplitude`: residues of the filter's modes.
All inputs are finite; a program needn't handle non-finite values.
Results may differ from a plain program's by a relative error of at most 0.0152.
Values may be sent and summed in bfloat16 or wider, within the bound.
No kernel may reach another device: no remote copies, remote signals or barrier semaphores. Data moves between devices by JAX's collectives and lax.ppermute only.
A program may use at most 128 MiB of HBM per device.

v0:
```python
import math

import jax
import jax.numpy as jnp
from jax import lax
from jax.sharding import PartitionSpec as P


def passed_along(shard, axis, by):
    count = lax.axis_size(axis)
    return lax.ppermute(shard, axis, [(i, (i + by) % count) for i in range(count)])


def unit_turn(step_index, period):
    residue = step_index % period
    nearest = jnp.minimum(residue, period - residue)
    angles = 2.0 * math.pi / period * nearest.astype(jnp.float32)
    cos_tab = jnp.cos(angles)
    sin_tab = jnp.sin(angles)
    sin_tab = jnp.where(2 * residue > period, -sin_tab, sin_tab)
    sin_tab = jnp.where((residue == 0) | (2 * residue == period), 0.0, sin_tab)
    return (cos_tab, sin_tab)


def forward_rows(a_values, wide, blocks):
    cos_tab, sin_tab = unit_turn(
        a_values[:, None] * jnp.arange(blocks, dtype=jnp.int32)[None, :], wide
    )
    return jnp.stack([cos_tab, -sin_tab]).astype(jnp.bfloat16)


def inverse_rows(a_values, wide, blocks):
    cos_tab, sin_tab = unit_turn(
        jnp.arange(blocks, dtype=jnp.int32)[:, None] * a_values[None, :], wide
    )
    return jnp.stack([cos_tab, -sin_tab]).astype(jnp.bfloat16)


def column_tables(a_values, seq_rows, period, wide):
    offsets = jnp.arange(seq_rows, dtype=jnp.int32)
    freq_index = a_values[:, None] + wide * offsets[None, :]
    cos_tab, sin_tab = unit_turn(offsets[None, :, None] * freq_index[:, None, :], period)
    cos_tab = cos_tab.astype(jnp.bfloat16)
    sin_tab = sin_tab.astype(jnp.bfloat16)
    fwd_table = jnp.stack(
        [jnp.stack([cos_tab, -sin_tab], axis=2), jnp.stack([sin_tab, cos_tab], axis=2)], axis=1
    )
    cos_back = jnp.swapaxes(cos_tab, 1, 2)
    sin_back = jnp.swapaxes(sin_tab, 1, 2)
    inv_table = jnp.stack(
        [jnp.stack([cos_back, sin_back], axis=2), jnp.stack([-sin_back, cos_back], axis=2)], axis=1
    )
    return (freq_index, fwd_table, inv_table)


def filter_spectrum(frequency, decay_rate, mode_gain, length, block_size):
    period = 2 * length
    retain = jnp.exp(-decay_rate)
    leakage = -jnp.expm1(-decay_rate)
    end_decay = jnp.exp(-decay_rate * length)
    end_leak = -jnp.expm1(-decay_rate * length)

    def one_block(freq_block):
        residue = freq_block % period
        nearest = jnp.minimum(residue, period - residue)
        sin_tab = unit_turn(freq_block, period)[1]
        half_sine = jnp.sin(math.pi / period * nearest.astype(jnp.float32))
        odd_freq = (residue % 2 == 1)[None, :, None]
        numerator = jnp.where(odd_freq, 1.0 + end_decay[:, None, :], end_leak[:, None, :])
        real_d = (
            leakage[:, None, :] + 2.0 * retain[:, None, :] * (half_sine * half_sine)[None, :, None]
        )
        imag_d = retain[:, None, :] * sin_tab[None, :, None]
        weighting = mode_gain[:, None, :] * numerator / (real_d * real_d + imag_d * imag_d)
        return (jnp.sum(weighting * real_d, axis=0), -jnp.sum(weighting * imag_d, axis=0))

    real_part, imag_part = lax.map(one_block, frequency.reshape(-1, block_size))
    channels = decay_rate.shape[1]
    return (real_part.reshape(-1, channels), imag_part.reshape(-1, channels))


def spectral_pass(
    lifted, freq_index, fwd_table, inv_table, decay_rate, mode_gain, length, block_size
):
    period = 2 * length
    forward_spec = jnp.einsum(
        "rxic,xriob->oxbc", lifted, fwd_table, preferred_element_type=jnp.float32
    )
    real_h, imag_h = filter_spectrum(
        freq_index.reshape(-1), decay_rate, mode_gain, length, block_size
    )
    real_h = real_h.reshape(forward_spec.shape[1:])
    imag_h = imag_h.reshape(forward_spec.shape[1:])
    product = jnp.stack(
        [
            (real_h * forward_spec[0] + imag_h * forward_spec[1]) / period,
            (real_h * forward_spec[1] - imag_h * forward_spec[0]) / period,
        ]
    ).astype(jnp.bfloat16)
    return jnp.einsum(
        "rxbc,xrboi->oxic", product, inv_table, preferred_element_type=jnp.float32
    ).astype(jnp.bfloat16)


def shards(gate, grad_out, decay, amplitude):
    blocks = lax.axis_size("ctx")
    seq_rows = gate.shape[1]
    channels = gate.shape[2]
    length = seq_rows * blocks
    period = 2 * length
    wide = 2 * blocks
    decay_rate = decay[0]
    mode_gain = amplitude[0]
    device_index = lax.axis_index("ctx")
    gated_grad = (gate[0].astype(jnp.float32) * grad_out[0].astype(jnp.float32)).astype(
        jnp.bfloat16
    )
    pieces = lax.all_to_all(
        gated_grad.reshape(1, seq_rows, channels), "ctx", split_axis=1, concat_axis=0, tiled=True
    )
    slots = jnp.arange(wide, dtype=jnp.int32)
    paired = slots // 2
    a_order = jnp.where(slots % 2 == 0, paired, jnp.where(paired == 0, blocks, wide - paired))
    lifted = jnp.einsum(
        "rap,pic->raic",
        forward_rows(a_order, wide, blocks),
        pieces,
        preferred_element_type=jnp.float32,
    ).astype(jnp.bfloat16)
    first_dev = device_index == 0
    spectrum = lax.all_to_all(lifted, "ctx", split_axis=1, concat_axis=2, tiled=True)
    own_freqs = jnp.stack([device_index, jnp.where(first_dev, blocks, wide - device_index)])
    freq_index, fwd_table, inv_table = column_tables(own_freqs, seq_rows, period, wide)
    spectral_out = spectral_pass(
        spectrum, freq_index, fwd_table, inv_table, decay_rate, mode_gain, length, 16
    )
    returned = lax.all_to_all(spectral_out, "ctx", split_axis=2, concat_axis=1, tiled=True)
    grad_rows = jnp.einsum(
        "raic,rpa->pic",
        returned,
        inverse_rows(a_order, wide, blocks),
        preferred_element_type=jnp.float32,
    ).astype(jnp.bfloat16)
    local_grad = lax.all_to_all(grad_rows, "ctx", split_axis=0, concat_axis=1, tiled=True)
    return passed_along(local_grad, "section", -1)


def solution(mesh):
    in_specs = (
        P("section", "ctx", None),
        P("section", "ctx", None),
        P("section", None, None),
        P("section", None, None),
    )
    out_specs = P("section", "ctx", None)
    return jax.shard_map(shards, mesh=mesh, in_specs=in_specs, out_specs=out_specs, check_vma=False)
```

profile of v0, /device:TPU:16, one launch (start us, length us, event | category | flops | bytes accessed | tf_op | source)
XLA Modules:
  0.0 715.2 jit_solution(3429673662714631453)
XLA Ops:
  1.8 2.4 copy.71
  4.7 7.0 reduce.2
  13.2 16.6 %all-to-all-start = ((bf16[64,2,4096]{2,1,0:T(2,128)(2,1)}), bf16[64,2,4096]{2,1,0:T(2,128)(2,1)}, u32[]{:S(2)}, u32[]{:S(2)}) async-start(bf16[64,2,4096]{2,1,0:T(2,128)(2,1)} %reshape.630), calls=%async_computation | async-start | bytes 2097152 | tf_op jit(solution)/shard_map/all_to_all | solution.py:118
  30.6 50.3 %all-to-all-done = bf16[64,2,4096]{2,1,0:T(2,128)(2,1)} async-done(((bf16[64,2,4096]{2,1,0:T(2,128)(2,1)}), bf16[64,2,4096]{2,1,0:T(2,128)(2,1)}, u32[]{:S(2)}, u32[]{:S(2)}) %all-to-all-start) | async-done | bytes 1048608 | tf_op jit(solution)/shard_map/all_to_all | solution.py:118
  80.9 6.5 reshape.631
  87.4 7.2 %bitcast_reduce_fusion = bf16[128,4096]{1,0:T(8,128)(2,1)} fusion(bf16[128,1,4096]{2,1,0:T(2,128)(2,1)S(1)} %reshape.631), kind=kLoop, calls=%fused_computation.140 | loop fusion | bytes 2097152 | tf_op jit(solution)/shard_map/all_to_all | solution.py:118
  96.6 3.8 convolution_convert_fusion
  100.4 8.5 %copy.39 = bf16[2,128,2,4096]{3,2,0,1:T(2,128)(2,1)} copy(bf16[2,128,2,4096]{3,1,2,0:T(8,128)(2,1)} %convolution_convert_fusion) | data formatting | bytes 8388608 | tf_op jit(solution)/shard_map/convert_element_type | solution.py:129
  108.9 9.0 %all-to-all-start.1 = ((bf16[2,128,2,4096]{3,2,0,1:T(2,128)(2,1)}), bf16[2,128,2,4096]{3,2,0,1:T(2,128)(2,1)}, u32[]{:S(2)}, u32[]{:S(2)}) async-start(bf16[2,128,2,4096]{3,2,0,1:T(2,128)(2,1)} %copy.39), calls=%async_computation.1 | async-start | bytes 8388608 | tf_op jit(solution)/shard_map/all_to_all | solution.py:131
  117.9 50.6 %while.15 = (s32[]{:T(128)}, f32[16,16,4096]{2,1,0:T(8,128)}, f32[16,16,4096]{2,1,0:T(8,128)}, f32[1,16,4096]{2,1,0:T(8,128)S(1)}, s32[16,16]{1,0:T(8,128)S(1)},...) while((s32[]{:T(128)}, f32[16,16,4096]{2,1,0:T(8,128)}, ...), condition=%wide.region_3.4_spmd, body=%wide.region_0.3_spmd.sunk | while | flops 13697618 | bytes 4194901 | solution.py:77
  118.1 2.2 fusion.69
  171.0 132.8 %all-to-all-done.1 = bf16[2,128,2,4096]{3,2,0,1:T(2,128)(2,1)} async-done(((bf16[2,128,2,4096]{3,2,0,1:T(2,128)(2,1)}), bf16[2,128,2,4096]{3,2,0,1:T(2,128)(2,1)}, u32[]{:S(2)}, u32[]{:S(2)}) %all-to-all-start.1) | async-done | bytes 4194336 | tf_op jit(solution)/shard_map/all_to_all | solution.py:131
  303.8 9.9 %copy.70 = bf16[2,64,2,2,4096]{4,3,1,0,2:T(2,128)(2,1)} copy(bf16[2,64,2,2,4096]{4,3,0,2,1:T(2,128)(2,1)} %bitcast.21) | data formatting | bytes 8388608 | tf_op jit(solution)/shard_map/all_to_all | solution.py:131
  313.7 7.2 %reshape.622 = bf16[2,2,128,4096,1]{3,2,0,1,4:T(8,128)(2,1)} reshape(bf16[2,2,64,2,4096]{4,3,2,0,1:T(2,128)(2,1)} %bitcast.94) | data formatting | bytes 8388608 | tf_op jit(solution)/shard_map/all_to_all | solution.py:131
  320.9 3.6 convolution_bitcast_fusion
  329.6 6.3 copy.43
  336.0 8.7 %all-to-all-start.2 = ((bf16[2,2,128,4096]{3,0,1,2:T(2,128)(2,1)}), bf16[2,2,128,4096]{3,0,1,2:T(2,128)(2,1)}, u32[]{:S(2)}, u32[]{:S(2)}) async-start(bf16[2,2,128,4096]{3,0,1,2:T(2,128)(2,1)} %copy.43), calls=%async_computation.2 | async-start | bytes 8388608 | tf_op jit(solution)/shard_map/all_to_all | solution.py:137
  344.8 185.7 %all-to-all-done.2 = bf16[2,2,128,4096]{3,0,1,2:T(2,128)(2,1)} async-done(((bf16[2,2,128,4096]{3,0,1,2:T(2,128)(2,1)}), bf16[2,2,128,4096]{3,0,1,2:T(2,128)(2,1)}, u32[]{:S(2)}, u32[]{:S(2)}) %all-to-all-start.2) | async-done | bytes 4194336 | tf_op jit(solution)/shard_map/all_to_all | solution.py:137
  530.5 9.4 %copy.69 = bf16[2,2,64,2,4096]{4,1,2,0,3:T(2,128)(2,1)} copy(bf16[2,2,64,2,4096]{4,0,1,3,2:T(2,128)(2,1)} %bitcast.32) | data formatting | bytes 8388608 | tf_op jit(solution)/shard_map/all_to_all | solution.py:137
  539.9 7.2 %all_to_all.53 = bf16[2,128,2,4096]{3,1,0,2:T(8,128)(2,1)} reshape(bf16[2,64,2,2,4096]{4,2,1,0,3:T(2,128)(2,1)} %bitcast.96) | data formatting | bytes 8388608 | tf_op jit(solution)/shard_map/all_to_all | solution.py:137
  547.1 3.0 fusion.8
  551.2 59.1 %all_to_all.60 = bf16[64,2,4096]{2,1,0:T(2,128)(2,1)S(1)} all-to-all(bf16[64,2,4096]{2,1,0:T(2,128)(2,1)S(1)} %copy.45), channel_id=1, replica_groups=mesh['ctx'=64,'section'=8] {'ctx'}, dimensions={0} | all-to-all | bytes 2097152 | tf_op jit(solution)/shard_map/all_to_all | solution.py:144
  610.8 10.4 %collective-permute-start = (bf16[1,128,4096]{2,1,0:T(8,128)(2,1)S(1)}, bf16[1,128,4096]{2,1,0:T(8,128)(2,1)S(1)}, u32[]{:S(2)}, u32[]{:S(2)}) collective-permute-start(bf16[1,128,4096]{2,1,0:T(8,128)(2,1)S(1)} %all_to_all.55), channel_id=1, source_target_pairs={{0,7},{1,0},{2,1},{3,2},{4,3},{5,4},{6,5},{7,6},{8,15},{9,8},{10,9... | collective-permute-start | bytes 3145736 | tf_op jit(solution)/shard_map/ppermute | solution.py:11
  621.2 92.8 %collective-permute-done = bf16[1,128,4096]{2,1,0:T(8,128)(2,1)S(1)} collective-permute-done((bf16[1,128,4096]{2,1,0:T(8,128)(2,1)S(1)}, bf16[1,128,4096]{2,1,0:T(8,128)(2,1)S(1)}, u32[]{:S(2)}, u32[]{:S(2)}) %collective-permute-start) | collective-permute-done | bytes 1048608 | tf_op jit(solution)/shard_map/ppermute | solution.py:11
  (130 shorter events, 64.6 us)
Async XLA Ops:
  4.2 26.2 %copy-start.3 = (f32[1,16,4096]{2,1,0:T(8,128)S(1)}, f32[1,16,4096]{2,1,0:T(8,128)}, u32[]{:S(2)}) copy-start(f32[1,16,4096]{2,1,0:T(8,128)} %param.8) | copy-start | bytes 786436
  13.2 67.6 %all-to-all-start = ((bf16[64,2,4096]{2,1,0:T(2,128)(2,1)}), bf16[64,2,4096]{2,1,0:T(2,128)(2,1)}, u32[]{:S(2)}, u32[]{:S(2)}) async-start(bf16[64,2,4096]{2,1,0:T(2,128)(2,1)} %reshape.630), calls=%async_computation | async-start | bytes 2097152 | tf_op jit(solution)/shard_map/all_to_all | solution.py:118
  108.9 9.0 %copy-start = (f32[1,16,4096]{2,1,0:T(8,128)S(1)}, f32[1,16,4096]{2,1,0:T(8,128)}, u32[]{:S(2)}) copy-start(f32[1,16,4096]{2,1,0:T(8,128)} %param.9) | copy-start | bytes 786436
  108.9 194.8 %all-to-all-start.1 = ((bf16[2,128,2,4096]{3,2,0,1:T(2,128)(2,1)}), bf16[2,128,2,4096]{3,2,0,1:T(2,128)(2,1)}, u32[]{:S(2)}, u32[]{:S(2)}) async-start(bf16[2,128,2,4096]{3,2,0,1:T(2,128)(2,1)} %copy.39), calls=%async_computation.1 | async-start | bytes 8388608 | tf_op jit(solution)/shard_map/all_to_all | solution.py:131
  320.9 3.6 copy-start.1
  320.9 4.7 copy-start.2
  336.0 194.5 %all-to-all-start.2 = ((bf16[2,2,128,4096]{3,0,1,2:T(2,128)(2,1)}), bf16[2,2,128,4096]{3,0,1,2:T(2,128)(2,1)}, u32[]{:S(2)}, u32[]{:S(2)}) async-start(bf16[2,2,128,4096]{3,0,1,2:T(2,128)(2,1)} %copy.43), calls=%async_computation.2 | async-start | bytes 8388608 | tf_op jit(solution)/shard_map/all_to_all | solution.py:137
  610.8 103.2 %collective-permute-start = (bf16[1,128,4096]{2,1,0:T(8,128)(2,1)S(1)}, bf16[1,128,4096]{2,1,0:T(8,128)(2,1)S(1)}, u32[]{:S(2)}, u32[]{:S(2)}) collective-permute-start(bf16[1,128,4096]{2,1,0:T(8,128)(2,1)S(1)} %all_to_all.55), channel_id=1, source_target_pairs={{0,7},{1,0},{2,1},{3,2},{4,3},{5,4},{6,5},{7,6},{8,15},{9,8},{10,9... | collective-permute-start | bytes 3145736 | tf_op jit(solution)/shard_map/ppermute | solution.py:11
where the time goes:
time: 724 us; the launch traced here: 715 us
  waiting for transfers between devices  462 us (64%)
  local copies, waits for them, and re-layouts  72.8 us (10%)
  other arithmetic  63.9 us (9%)
  blocking collectives  59.1 us (8%)
  starting transfers between devices  44.7 us (6%)
  matrix products  12.1 us (2%)
    all_to_all x1, waiting for transfers between devices, shards(): lax.all_to_all(spectral_out, 'ctx', split_axis=2, concat_axis=1, tiled=True)  186 us
    all_to_all x1, waiting for transfers between devices, shards(): lax.all_to_all(lifted, 'ctx', split_axis=1, concat_axis=2, tiled=True)  133 us
    ppermute x1, waiting for transfers between devices, passed_along(): lax.ppermute(shard, axis, [(i, (i + by) % count) for i in range(count)])  92.8 us
    all_to_all x1, blocking collectives, shards(): lax.all_to_all(grad_rows, 'ctx', split_axis=0, concat_axis=1, tiled=True)  59.1 us
    all_to_all x1, waiting for transfers between devices, shards(): lax.all_to_all(gated_grad.reshape(1, seq_rows, channels), 'ctx', split_ax...  50.3 us
    reduce_sum x16, other arithmetic, one_block(): jnp.sum(weighting * imag_d, axis=0)  34.9 us
    all_to_all x2, local copies, waits for them, and re-layouts, shards(): lax.all_to_all(lifted, 'ctx', split_axis=1, concat_axis=2, tiled=True)  17.1 us
    all_to_all x1, starting transfers between devices, shards(): lax.all_to_all(gated_grad.reshape(1, seq_rows, channels), 'ctx', split_ax...  16.6 us
  transfers between devices with their start and end apart: 4, of which 4 were waited for; matrix products, arithmetic and copies ran while one was open for 7% of the time, Pallas kernels for 0%

commit v1 on v0

v1 whole, which is shorter than its diff:
```python
import functools

import jax
import jax.numpy as jnp
from jax import lax
from jax.experimental import pallas as pl
from jax.experimental.pallas import tpu as pltpu
from jax.sharding import Mesh, PartitionSpec as P

MODES = 16
ROWS = 128
CHIP_RUN = 8
F32 = jnp.float32


def gated_rows(gate, grad):
    return (gate.astype(F32) * grad.astype(F32)).astype(jnp.bfloat16).astype(F32)


def lanes_of(group):
    return pl.ds(pl.multiple_of(group * 128, 128), 128)


def spread(row):
    return jnp.broadcast_to(row, (8, 128))


def state_kernel(gate_ref, grad_ref, decay_ref, state_ref):
    sub = lax.broadcasted_iota(jnp.int32, (8, 128), 0).astype(F32)

    def one_group(group, _):
        lanes = lanes_of(group)
        rates = [spread(decay_ref[j : j + 1, lanes]) for j in range(MODES)]
        leap = [jnp.exp(-8.0 * r) for r in rates]
        held = [None] * MODES
        for pair in reversed(range(ROWS // 16)):
            rows = slice(16 * pair, 16 * pair + 16)
            both = gated_rows(gate_ref[rows, lanes], grad_ref[rows, lanes])
            for part in (both[8:16], both[0:8]):
                held = [part if h is None else h * q + part for h, q in zip(held, leap)]
        for j in range(MODES):
            total = jnp.sum(held[j] * jnp.exp(-rates[j] * sub), axis=0, keepdims=True)
            state_ref[j // 2, j % 2 : j % 2 + 1, lanes] = total
        return 0

    lax.fori_loop(0, state_ref.shape[2] // 128, one_group, 0)


def block_states(gate, grad, decay, width=1024):
    channels = gate.shape[1]
    wide = lambda c: (0, c)
    return pl.pallas_call(
        state_kernel,
        grid=(channels // width,),
        in_specs=[
            pl.BlockSpec((ROWS, width), wide),
            pl.BlockSpec((ROWS, width), wide),
            pl.BlockSpec((MODES, width), wide),
        ],
        out_specs=pl.BlockSpec((MODES // 2, 2, width), lambda c: (0, 0, c)),
        out_shape=jax.ShapeDtypeStruct((MODES // 2, 2, channels), F32),
        name="block_states",
    )(gate, grad, decay)


def plane_kernel(state_ref, rate_ref, total_ref):
    step = jnp.exp(-float(ROWS) * rate_ref[...])
    total = state_ref[CHIP_RUN - 1]
    for k in reversed(range(CHIP_RUN - 1)):
        total = total * step + state_ref[k]
    for k in range(CHIP_RUN):
        total_ref[k] = total


def plane_totals(states, rates):
    return pl.pallas_call(
        plane_kernel,
        out_shape=jax.ShapeDtypeStruct(states.shape, F32),
        name="plane_totals",
    )(states, rates)


def entry_kernel(plane_ref, state_ref, total_ref, rate_ref, entry_ref):
    plane = plane_ref[0]
    rates = rate_ref[...]
    step = jnp.exp(-float(ROWS) * rates)
    stride = jnp.exp(-float(ROWS * CHIP_RUN) * rates)
    carry = jnp.zeros_like(rates)
    for z in reversed(range(1, CHIP_RUN)):
        carry = jnp.where(z > plane, carry * stride + total_ref[z], carry)
    for k in reversed(range(CHIP_RUN)):
        entry_ref[k] = carry
        carry = carry * step + state_ref[k]


def block_entries(plane, states, totals, rates):
    whole = pl.BlockSpec(memory_space=pltpu.VMEM)
    return pl.pallas_call(
        entry_kernel,
        in_specs=[pl.BlockSpec(memory_space=pltpu.SMEM), whole, whole, whole],
        out_shape=jax.ShapeDtypeStruct(states.shape, F32),
        name="block_entries",
    )(plane, states, totals, rates)


def sweep_kernel(gate_ref, grad_ref, entry_ref, decay_ref, gain_ref, out_ref, source, result):
    sub = lax.broadcasted_iota(jnp.int32, (8, 128), 0)

    def one_group(group, _):
        lanes = lanes_of(group)
        for pair in range(ROWS // 16):
            rows = slice(16 * pair, 16 * pair + 16)
            source[rows, :] = gated_rows(gate_ref[rows, lanes], grad_ref[rows, lanes])
        rates = [spread(decay_ref[j : j + 1, lanes]) for j in range(MODES)]
        keep = [jnp.exp(-r) for r in rates]
        held = [None] * MODES
        for i in reversed(range(16)):
            part = source[pl.ds(i, 8, stride=16), :]
            held = [part if h is None else h * q + part for h, q in zip(held, keep)]
        for j in range(MODES):
            enter = spread(entry_ref[j // 2, j % 2 : j % 2 + 1, lanes])
            value = jnp.where(sub == 7, enter, pltpu.roll(held[j], 7, 0))
            for shift in (1, 2, 4):
                leap = jnp.where(sub < 8 - shift, jnp.exp(-16.0 * shift * rates[j]), 0.0)
                value = value + leap * pltpu.roll(value, 8 - shift, 0)
            held[j] = value
        gains = [spread(gain_ref[j : j + 1, lanes]) for j in range(MODES)]
        for i in reversed(range(16)):
            part = source[pl.ds(i, 8, stride=16), :]
            held = [h * q + part for h, q in zip(held, keep)]
            terms = [h * a for h, a in zip(held, gains)]
            while len(terms) > 1:
                terms = [a + b for a, b in zip(terms[::2], terms[1::2])]
            result[pl.ds(i, 8, stride=16), :] = terms[0]
        for pair in range(ROWS // 16):
            rows = slice(16 * pair, 16 * pair + 16)
            out_ref[rows, lanes] = result[rows, :].astype(jnp.bfloat16)
        return 0

    lax.fori_loop(0, out_ref.shape[1] // 128, one_group, 0)


def sweep(gate, grad, entries, decay, gain, width=1024):
    channels = gate.shape[1]
    wide = lambda c: (0, c)
    return pl.pallas_call(
        sweep_kernel,
        grid=(channels // width,),
        in_specs=[
            pl.BlockSpec((ROWS, width), wide),
            pl.BlockSpec((ROWS, width), wide),
            pl.BlockSpec((MODES // 2, 2, width), lambda c: (0, 0, c)),
            pl.BlockSpec((MODES, width), wide),
            pl.BlockSpec((MODES, width), wide),
        ],
        out_specs=pl.BlockSpec((ROWS, width), wide),
        out_shape=jax.ShapeDtypeStruct((ROWS, channels), jnp.bfloat16),
        scratch_shapes=[pltpu.VMEM((ROWS, 128), F32), pltpu.VMEM((ROWS, 128), F32)],
        name="sweep",
    )(gate, grad, entries, decay, gain)


def exchange(values, axis):
    return lax.all_to_all(values, axis, split_axis=0, concat_axis=0, tiled=True)


def passed_along(shard, axis, by):
    count = lax.axis_size(axis)
    return lax.ppermute(shard, axis, [(i, (i + by) % count) for i in range(count)])


def shards(gate, grad, decay, amplitude):
    gate, grad, decay, gain = gate[0], grad[0], decay[0], amplitude[0]
    place = lax.axis_index("place")
    plane = lax.axis_index("plane").reshape(1)
    own_rates = lax.dynamic_slice_in_dim(decay, 2 * place, 2, axis=0)
    states = exchange(block_states(gate, grad, decay), "place")
    totals = exchange(plane_totals(states, own_rates), "plane")
    entries = exchange(block_entries(plane, states, totals, own_rates), "place")
    local = sweep(gate, grad, entries, decay, gain)
    return passed_along(local, "section", -1)[None]


def solution(mesh):
    sections = mesh.shape["section"]
    parts = Mesh(
        mesh.devices.reshape(CHIP_RUN, CHIP_RUN, sections), ("plane", "place", "section")
    )
    rows = P("section", ("plane", "place"), None)
    params = P("section", None, None)
    return jax.shard_map(
        shards,
        mesh=parts,
        in_specs=(rows, rows, params, params),
        out_specs=rows,
        check_vma=False,
    )
```

time: 724 us -> 179 us (0.25)
  the two profiles are of different devices: /device:TPU:16 before, /device:TPU:37 now
where the time goes in v1:
time: 179 us; the launch traced here: 178 us
  waiting for transfers between devices  112 us (63%)
  starting transfers between devices  25.1 us (14%)
  Pallas kernels  21.4 us (12%)
  blocking collectives  16.1 us (9%)
  local copies, waits for them, and re-layouts  3.9 us (2%)
    ppermute x1, waiting for transfers between devices, passed_along(): lax.ppermute(shard, axis, [(i, (i + by) % count) for i in range(count)])  94.6 us
    all_to_all x2, starting transfers between devices, exchange(): return lax.all_to_all(values, axis, split_axis=0, concat_axis=0, tiled=True)  17.2 us
    all_to_all x2, waiting for transfers between devices, exchange(): return lax.all_to_all(values, axis, split_axis=0, concat_axis=0, tiled=True)  16.9 us
    all_to_all x1, blocking collectives, exchange(): return lax.all_to_all(values, axis, split_axis=0, concat_axis=0, tiled=True)  16.1 us
    pallas_call x1, Pallas kernels, sweep(): pl.pallas_call(sweep_kernel, grid=(channels // width,), in_specs=[pl.Bloc...  12.2 us
    ppermute x1, starting transfers between devices, passed_along(): lax.ppermute(shard, axis, [(i, (i + by) % count) for i in range(count)])  7.9 us
    pallas_call x1, Pallas kernels, block_states(): pl.pallas_call(state_kernel, grid=(channels // width,), in_specs=[pl.Bloc...  5.69 us
  transfers between devices with their start and end apart: 3, of which 3 were waited for; matrix products, arithmetic and copies ran while one was open for 1% of the time, Pallas kernels for 0%

profile of v1, /device:TPU:37, one launch (start us, length us, event | category | flops | bytes accessed | tf_op | source)
XLA Modules:
  0.0 178.0 jit_solution(11978870913923991248)
XLA Ops:
  0.0 5.7 %block_states.1 = f32[8,2,4096]{2,1,0:T(2,128)} custom-call(bf16[128,4096]{1,0:T(8,128)(2,1)} %bitcast.8, bf16[128,4096]{1,0:T(8,128)(2,1)} %bitcast.10, f32[16,4096]{1,0:T(8,128)} %bitcast.12), custom_call_target="tpu_custom_call" | custom-call | tf_op jit(solution)/shard_map/block_states/pallas_call | solution.py:52
  5.7 5.1 %all-to-all-start = ((f32[8,2,4096]{2,1,0:T(2,128)}), f32[8,2,4096]{2,1,0:T(2,128)S(1)}, u32[]{:S(2)}, u32[]{:S(2)}) async-start(f32[8,2,4096]{2,1,0:T(2,128)} %block_states.1), calls=%async_computation | async-start | bytes 524288 | tf_op jit(solution)/shard_map/all_to_all | solution.py:164
  10.8 1.5 dynamic-slice_bitcast_fusion.rate_ref
  12.4 5.0 %all-to-all-done.state_ref = f32[8,2,4096]{2,1,0:T(2,128)S(1)} async-done(((f32[8,2,4096]{2,1,0:T(2,128)}), f32[8,2,4096]{2,1,0:T(2,128)S(1)}, u32[]{:S(2)}, u32[]{:S(2)}) %all-to-all-start) | async-done | bytes 262176 | tf_op jit(solution)/shard_map/all_to_all | solution.py:164
  17.3 0.0 copy-start
  17.3 0.7 copy-done
  18.0 1.7 plane_totals.1
  19.7 12.1 %all-to-all-start.1 = ((f32[8,2,4096]{2,1,0:T(2,128)}), f32[8,2,4096]{2,1,0:T(2,128)S(1)}, u32[]{:S(2)}, u32[]{:S(2)}) async-start(f32[8,2,4096]{2,1,0:T(2,128)} %plane_totals.1), calls=%async_computation.1 | async-start | bytes 524288 | tf_op jit(solution)/shard_map/all_to_all | solution.py:164
  31.8 12.0 %all-to-all-done.1.total_ref = f32[8,2,4096]{2,1,0:T(2,128)S(1)} async-done(((f32[8,2,4096]{2,1,0:T(2,128)}), f32[8,2,4096]{2,1,0:T(2,128)S(1)}, u32[]{:S(2)}, u32[]{:S(2)}) %all-to-all-start.1) | async-done | bytes 262176 | tf_op jit(solution)/shard_map/all_to_all | solution.py:164
  43.8 0.0 copy-start.1
  43.8 0.7 copy-done.1
  44.5 1.8 %block_entries.1 = f32[8,2,4096]{2,1,0:T(2,128)} custom-call(s32[1]{0:T(128)} %bitcast.2.plane_ref, f32[8,2,4096]{2,1,0:T(2,128)} %copy-done, f32[8,2,4096]{2,1,0:T(2,128)} %copy-done.1, f32[2,4096]{1,0:T(2,128)} %dynamic-slice_bitcast_fusion.rate_ref), custom_call_target="tpu_custom_call" | custom-call | tf_op jit(solution)/shard_map/block_entries/pallas_call | solution.py:98
  46.3 16.1 %all_to_all.15.entry_ref = f32[8,2,4096]{2,1,0:T(2,128)} all-to-all(f32[8,2,4096]{2,1,0:T(2,128)} %block_entries.1), channel_id=1, replica_groups=mesh['plane'=8,'place'=8,'section'=8] {'place'}, dimensions={0} | all-to-all | bytes 524288 | tf_op jit(solution)/shard_map/all_to_all | solution.py:164
  62.3 12.2 %sweep.1 = bf16[128,4096]{1,0:T(8,128)(2,1)} custom-call(bf16[128,4096]{1,0:T(8,128)(2,1)} %bitcast.9, bf16[128,4096]{1,0:T(8,128)(2,1)} %bitcast.11, f32[8,2,4096]{2,1,0:T(2,128)} %all_to_all.15.entry_ref, f32[16,4096]{1,0:T(8,128)} %bitcast.13, f32[16,4096]{1,0:T(8,128)} %bitcast.15), custom_call_target="tpu_custom_call" | custom-call | tf_op jit(solution)/shard_map/sweep/pallas_call | solution.py:146
  74.5 7.9 %collective-permute-start = (bf16[128,4096]{1,0:T(8,128)(2,1)}, bf16[128,4096]{1,0:T(8,128)(2,1)S(1)}, u32[]{:S(2)}, u32[]{:S(2)}) collective-permute-start(bf16[128,4096]{1,0:T(8,128)(2,1)} %sweep.1), channel_id=1, source_target_pairs={{0,7},{1,0},{2,1},{3,2},{4,3},{5,4},{6,5},{7,6},{8,15},{9,8},{10,9... | collective-permute-start | bytes 3145736 | tf_op jit(solution)/shard_map/ppermute | solution.py:169
  82.4 94.6 %collective-permute-done = bf16[128,4096]{1,0:T(8,128)(2,1)S(1)} collective-permute-done((bf16[128,4096]{1,0:T(8,128)(2,1)}, bf16[128,4096]{1,0:T(8,128)(2,1)S(1)}, u32[]{:S(2)}, u32[]{:S(2)}) %collective-permute-start) | collective-permute-done | bytes 1048608 | tf_op jit(solution)/shard_map/ppermute | solution.py:169
  177.1 1.0 copy.6
Async XLA Ops:
  5.7 11.6 %all-to-all-start = ((f32[8,2,4096]{2,1,0:T(2,128)}), f32[8,2,4096]{2,1,0:T(2,128)S(1)}, u32[]{:S(2)}, u32[]{:S(2)}) async-start(f32[8,2,4096]{2,1,0:T(2,128)} %block_states.1), calls=%async_computation | async-start | bytes 524288 | tf_op jit(solution)/shard_map/all_to_all | solution.py:164
  17.3 0.7 copy-start
  19.7 24.0 %all-to-all-start.1 = ((f32[8,2,4096]{2,1,0:T(2,128)}), f32[8,2,4096]{2,1,0:T(2,128)S(1)}, u32[]{:S(2)}, u32[]{:S(2)}) async-start(f32[8,2,4096]{2,1,0:T(2,128)} %plane_totals.1), calls=%async_computation.1 | async-start | bytes 524288 | tf_op jit(solution)/shard_map/all_to_all | solution.py:164
  43.8 0.7 copy-start.1
  74.5 102.5 %collective-permute-start = (bf16[128,4096]{1,0:T(8,128)(2,1)}, bf16[128,4096]{1,0:T(8,128)(2,1)S(1)}, u32[]{:S(2)}, u32[]{:S(2)}) collective-permute-start(bf16[128,4096]{1,0:T(8,128)(2,1)} %sweep.1), channel_id=1, source_target_pairs={{0,7},{1,0},{2,1},{3,2},{4,3},{5,4},{6,5},{7,6},{8,15},{9,8},{10,9... | collective-permute-start | bytes 3145736 | tf_op jit(solution)/shard_map/ppermute | solution.py:169

commit v2 on v1

v2 whole, which is shorter than its diff:
```python
import functools

import jax
import jax.numpy as jnp
from jax import lax
from jax.experimental import pallas as pl
from jax.experimental.pallas import tpu as pltpu
from jax.sharding import Mesh, PartitionSpec as P

MODES = 16
ROWS = 128
PLACES = 8
SLOT = MODES // PLACES
PLANES = 64 // PLACES
EARLY = 2048
WIDTH = 1024
HALF = PLANES // 2
F32 = jnp.float32


def gated_rows(gate, grad):
    return (gate.astype(F32) * grad.astype(F32)).astype(jnp.bfloat16).astype(F32)


def lanes_of(group):
    return pl.ds(pl.multiple_of(group * 128, 128), 128)


def mode_row(ref, j, lanes):
    row = ref[j : j + 1, lanes] if len(ref.shape) == 2 else ref[j // SLOT, j % SLOT : j % SLOT + 1, lanes]
    return jnp.broadcast_to(row, (8, 128))


def source_rows(refs, rows, lanes):
    if len(refs) == 1:
        return refs[0][rows, lanes].astype(F32)
    return gated_rows(refs[0][rows, lanes], refs[1][rows, lanes])


def columns(shape, first=0):
    lead = (0,) * (len(shape) - 1)
    skip = first // WIDTH
    return pl.BlockSpec(shape[:-1] + (WIDTH,), lambda c: lead + (c + skip,))


def in_parts(kernel, sources, counts):
    def body(*refs):
        if len(counts) == 1:
            return kernel(refs[:sources], *refs[sources:])
        step, start = pl.program_id(0), 0
        for source, count in zip(refs[:sources], counts):
            pl.when((step >= start) & (step < start + count))(
                functools.partial(kernel, (source,), *refs[sources:])
            )
            start += count

    return body


def part_columns(parts):
    specs, start = [], 0
    for part in parts:
        count = part.shape[1] // WIDTH
        specs.append(
            pl.BlockSpec(
                (ROWS, WIDTH), lambda c, s=start, n=count: (0, jnp.clip(c - s, 0, n - 1))
            )
        )
        start += count
    return specs, [part.shape[1] // WIDTH for part in parts]


def state_kernel(sources, decay_ref, state_ref):
    sub = lax.broadcasted_iota(jnp.int32, (8, 128), 0).astype(F32)

    def one_group(group, _):
        lanes = lanes_of(group)
        rates = [mode_row(decay_ref, j, lanes) for j in range(MODES)]
        leap = [jnp.exp(-8.0 * r) for r in rates]
        held = [None] * MODES
        for pair in reversed(range(ROWS // 16)):
            both = source_rows(sources, slice(16 * pair, 16 * pair + 16), lanes)
            for part in (both[8:16], both[0:8]):
                held = [part if h is None else h * q + part for h, q in zip(held, leap)]
        for j in range(MODES):
            total = jnp.sum(held[j] * jnp.exp(-rates[j] * sub), axis=0, keepdims=True)
            state_ref[j // SLOT, j % SLOT : j % SLOT + 1, lanes] = total
        return 0

    lax.fori_loop(0, state_ref.shape[2] // 128, one_group, 0)


def all_states(gate, grad, decay, width=1024):
    channels = gate.shape[1]
    wide = lambda c: (0, c)
    return pl.pallas_call(
        in_parts(state_kernel, 2, [1]),
        grid=(channels // width,),
        in_specs=[pl.BlockSpec((n, width), wide) for n in (ROWS, ROWS, MODES)],
        out_specs=pl.BlockSpec((PLACES, SLOT, width), lambda c: (0, 0, c)),
        out_shape=jax.ShapeDtypeStruct((PLACES, SLOT, channels), F32),
        name="all_states",
    )(gate, grad, decay)


def early_states(parts, decay, decay_first):
    specs, counts = part_columns(parts)
    return pl.pallas_call(
        in_parts(state_kernel, len(parts), counts),
        grid=(sum(counts),),
        in_specs=specs + [columns(decay.shape, decay_first)],
        out_specs=columns((PLACES, SLOT, EARLY)),
        out_shape=jax.ShapeDtypeStruct((PLACES, SLOT, EARLY), F32),
        name="early_states",
    )(*parts, decay)


def plane_kernel(state_ref, rate_ref, gain_ref, sum_ref, full_ref, entry_ref):
    channels = rate_ref.shape[1]
    step = jnp.exp(-float(ROWS) * rate_ref[...])
    total = jnp.zeros_like(step)
    for k in reversed(range(PLACES)):
        entry_ref[k] = total[:, EARLY:]
        total = total * step + state_ref[k]
    for ref in (sum_ref, full_ref):
        ref[:, :EARLY] = total[:, :EARLY]
        ref[:, EARLY:channels] = total[:, EARLY:] * gain_ref[:, EARLY:]
    full_ref[:, channels : 2 * channels] = rate_ref[...]
    full_ref[:, 2 * channels :] = gain_ref[:, :EARLY]


def plane_sums(states, rates, gains):
    channels = rates.shape[1]
    return pl.pallas_call(
        plane_kernel,
        out_shape=[
            jax.ShapeDtypeStruct((SLOT, channels), F32),
            jax.ShapeDtypeStruct((SLOT, 2 * channels + EARLY), F32),
            jax.ShapeDtypeStruct((PLACES, SLOT, channels - EARLY), F32),
        ],
        name="plane_sums",
    )(states, rates, gains)


def entry_kernel(plane_ref, state_ref, full_ref, *refs):
    sum_refs, entry_ref = refs[:-1], refs[-1]
    channels = entry_ref.shape[2]
    rates = full_ref[:, channels : 2 * channels]
    stride = jnp.exp(-float(ROWS * PLACES) * rates)
    middle = jnp.where(plane_ref[0] < PLANES - HALF, full_ref[:, :channels], 0.0)
    values = [ref[...] for ref in sum_refs]
    values.insert(HALF - 1, middle)
    carry = values.pop()
    while values:
        carry = carry * stride + values.pop()
    step = jnp.exp(-float(ROWS) * rates)
    early, late = carry[:, :EARLY], carry[:, EARLY:]
    for k in reversed(range(PLACES)):
        entry_ref[k, :, :EARLY] = early
        entry_ref[k, :, EARLY:] = late
        early = early * step[:, :EARLY] + state_ref[k]
        late = late * step[:, EARLY:]


def block_entries(plane, states, full, sums):
    whole = pl.BlockSpec(memory_space=pltpu.VMEM)
    return pl.pallas_call(
        entry_kernel,
        in_specs=[pl.BlockSpec(memory_space=pltpu.SMEM)] + [whole] * (2 + len(sums)),
        out_shape=jax.ShapeDtypeStruct((PLACES, SLOT, sums[0].shape[1]), F32),
        name="block_entries",
    )(plane, states, full, *sums)


def sweep_kernel(sources, entry_ref, decay_ref, gain_ref, out_ref, source, result):
    sub = lax.broadcasted_iota(jnp.int32, (8, 128), 0)

    def one_group(group, _):
        lanes = lanes_of(group)
        for pair in range(ROWS // 16):
            rows = slice(16 * pair, 16 * pair + 16)
            source[rows, :] = source_rows(sources, rows, lanes)
        rates = [mode_row(decay_ref, j, lanes) for j in range(MODES)]
        keep = [jnp.exp(-r) for r in rates]
        held = [None] * MODES
        for i in reversed(range(16)):
            part = source[pl.ds(i, 8, stride=16), :]
            held = [part if h is None else h * q + part for h, q in zip(held, keep)]
        for j in range(MODES):
            value = jnp.where(sub == 7, mode_row(entry_ref, j, lanes), pltpu.roll(held[j], 7, 0))
            for shift in (1, 2, 4):
                leap = jnp.where(sub < 8 - shift, jnp.exp(-16.0 * shift * rates[j]), 0.0)
                value = value + leap * pltpu.roll(value, 8 - shift, 0)
            held[j] = value
        gains = [mode_row(gain_ref, j, lanes) for j in range(MODES)]
        for i in reversed(range(16)):
            part = source[pl.ds(i, 8, stride=16), :]
            held = [h * q + part for h, q in zip(held, keep)]
            terms = [h * a for h, a in zip(held, gains)]
            while len(terms) > 1:
                terms = [a + b for a, b in zip(terms[::2], terms[1::2])]
            result[pl.ds(i, 8, stride=16), :] = terms[0]
        for pair in range(ROWS // 16):
            rows = slice(16 * pair, 16 * pair + 16)
            out_ref[rows, lanes] = result[rows, :].astype(jnp.bfloat16)
        return 0

    lax.fori_loop(0, WIDTH // 128, one_group, 0)


def sweep(sources, specs, counts, params, channels, out_channels):
    return pl.pallas_call(
        in_parts(sweep_kernel, len(sources), counts),
        grid=(channels // WIDTH,),
        in_specs=specs + [columns(a.shape, first) for a, first in params],
        out_specs=columns((ROWS, out_channels)),
        out_shape=jax.ShapeDtypeStruct((ROWS, out_channels), jnp.bfloat16),
        scratch_shapes=[pltpu.VMEM((ROWS, 128), F32), pltpu.VMEM((ROWS, 128), F32)],
        name="sweep",
    )(*sources, *(a for a, _ in params))


def finish_kernel(_, late_ref, entry_ref, decay_ref, out_ref):
    ahead = 8.0 - lax.broadcasted_iota(jnp.int32, (8, 128), 0).astype(F32)

    def one_group(group, _):
        lanes = lanes_of(group)
        rates = [mode_row(decay_ref, j, lanes) for j in range(MODES)]
        leap = [jnp.exp(-8.0 * r) for r in rates]
        held = [
            mode_row(entry_ref, j, lanes) * jnp.exp(-r * ahead) for j, r in enumerate(rates)
        ]
        for pair in reversed(range(ROWS // 16)):
            rows = slice(16 * pair, 16 * pair + 16)
            halves = []
            for _ in range(2):
                terms = held
                while len(terms) > 1:
                    terms = [a + b for a, b in zip(terms[::2], terms[1::2])]
                halves.append(terms[0])
                held = [h * q for h, q in zip(held, leap)]
            whole = jnp.concatenate(halves[::-1], axis=0)
            out_ref[rows, lanes] = (late_ref[rows, lanes].astype(F32) + whole).astype(jnp.bfloat16)
        return 0

    lax.fori_loop(0, WIDTH // 128, one_group, 0)


def finish_late(out, late_rows, entries, decay):
    late = late_rows.shape[1]
    return pl.pallas_call(
        finish_kernel,
        grid=(late // WIDTH,),
        in_specs=[
            pl.BlockSpec(memory_space=pl.ANY),
            columns(late_rows.shape),
            columns(entries.shape, EARLY),
            columns(decay.shape, EARLY),
        ],
        out_specs=columns(out.shape, EARLY),
        out_shape=pltpu.HBM(out.shape, out.dtype),
        input_output_aliases={0: 0},
        name="finish_late",
    )(out, late_rows, entries, decay)


def exchange(values, axis):
    return lax.all_to_all(values, axis, split_axis=0, concat_axis=0, tiled=True)


def passed_along(shard, axis, by):
    count = lax.axis_size(axis)
    return lax.ppermute(shard, axis, [(i, (i + by) % count) for i in range(count)])


def as_one_step(always, step, *args):
    shapes = jax.eval_shape(step, *args)
    empty = lambda *_: jax.tree.map(lambda a: jnp.zeros(a.shape, a.dtype), shapes)
    return lax.cond(always, step, empty, *args)


def from_plane(message, by, ring):
    planes, sections = lax.axis_size("plane"), lax.axis_size("section")
    pairs = [
        (z * sections + s, (z - by) % planes * sections + (s - 1) % sections)
        for z in range(0 if ring else by, planes)
        for s in range(sections)
    ]
    return lax.ppermute(message, ("plane", "section"), pairs)


def late_step(gate, grad, decay, gain):
    late = gate.shape[1] - EARLY
    first = SLOT * lax.axis_index("place")
    rates = lax.dynamic_slice_in_dim(decay, first, SLOT, axis=0)
    gains = lax.dynamic_slice_in_dim(gain, first, SLOT, axis=0)
    states = exchange(all_states(gate, grad, decay), "place")
    total, full, entries = plane_sums(states, rates, gains)
    full = from_plane(full, HALF, True)
    sums = [from_plane(total, k, False) for k in range(1, HALF)]
    total, full, *sums = lax.optimization_barrier((total, full, *sums))
    sums += [from_plane(total, k, False) for k in range(HALF + 1, PLANES)]
    entries = exchange(entries, "place")
    sources = [gate, grad]
    specs = [columns(s.shape, EARLY) for s in sources]
    params = [(entries, 0), (decay, EARLY), (gain, EARLY)]
    return sweep(sources, specs, [1], params, late, late), full, sums


def early_step(plane, gated, full, sums):
    channels = sums[0].shape[1]
    specs, counts = part_columns([gated])
    params = jnp.broadcast_to(full[None, :, channels:], (PLACES, SLOT, channels + EARLY))
    params = exchange(params, "place")
    states = exchange(early_states([gated], params, 0), "place")
    entries = exchange(block_entries(plane, states, full, sums), "place")
    columns_of = [(entries, 0), (params, 0), (params, channels)]
    return sweep([gated], specs, counts, columns_of, EARLY, channels), entries, params


def shards(gate, grad, decay, amplitude):
    gate, grad, decay, gain = gate[0], grad[0], decay[0], amplitude[0]
    always = lax.axis_index("place") >= 0
    plane = lax.axis_index("plane").reshape(1)
    gated = (gate[:, :EARLY].astype(F32) * grad[:, :EARLY].astype(F32)).astype(jnp.bfloat16)
    arrived = passed_along(gated, "section", -1)
    gate, grad, gated = lax.optimization_barrier((gate, grad, gated))
    local, full, sums = as_one_step(always, late_step, gate, grad, decay, gain)
    late_rows = passed_along(local, "section", -1)
    out, entries, params = as_one_step(always, early_step, plane, arrived, full, sums)
    return finish_late(out, late_rows, entries, params)[None]


def solution(mesh):
    sections = mesh.shape["section"]
    parts = Mesh(mesh.devices.reshape(PLANES, PLACES, sections), ("plane", "place", "section"))
    rows = P("section", ("plane", "place"), None)
    params = P("section", None, None)
    return jax.shard_map(
        shards,
        mesh=parts,
        in_specs=(rows, rows, params, params),
        out_specs=rows,
        check_vma=False,
    )
```

time: 179 us -> 161 us (0.90)
  the two profiles are of different devices: /device:TPU:37 before, /device:TPU:64 now
where the time goes in v2:
time: 161 us; the launch traced here: 160 us
  starting transfers between devices  63.3 us (39%)
  blocking collectives  34 us (21%)
  Pallas kernels  28.6 us (18%)
  waiting for transfers between devices  27.1 us (17%)
  local copies, waits for them, and re-layouts  4.06 us (3%)
  other arithmetic  2.24 us (1%)
    ppermute x2, starting transfers between devices, passed_along(): lax.ppermute(shard, axis, [(i, (i + by) % count) for i in range(count)])  37.4 us
    all_to_all x3, blocking collectives, exchange(): return lax.all_to_all(values, axis, split_axis=0, concat_axis=0, tiled=True)  34 us
    ppermute x7, waiting for transfers between devices, from_plane(): return lax.ppermute(message, ('plane', 'section'), pairs)  20.3 us
    ppermute x7, starting transfers between devices, from_plane(): return lax.ppermute(message, ('plane', 'section'), pairs)  18 us
    pallas_call x2, Pallas kernels, sweep(): pl.pallas_call(in_parts(sweep_kernel, len(sources), counts), grid=(channe...  13 us
    all_to_all x2, starting transfers between devices, exchange(): return lax.all_to_all(values, axis, split_axis=0, concat_axis=0, tiled=True)  7.98 us
    all_to_all x2, waiting for transfers between devices, exchange(): return lax.all_to_all(values, axis, split_axis=0, concat_axis=0, tiled=True)  6.88 us
    pallas_call x1, Pallas kernels, all_states(): pl.pallas_call(in_parts(state_kernel, 2, [1]), grid=(channels // width,),...  5.61 us
  transfers between devices with their start and end apart: 11, of which 5 were waited for; matrix products, arithmetic and copies ran while one was open for 1% of the time, Pallas kernels for 16%

profile of v2, /device:TPU:64, one launch (start us, length us, event | category | flops | bytes accessed | tf_op | source)
XLA Modules:
  0.0 159.5 jit_solution(15362693725487759652)
XLA Ops:
  0.0 2.2 %multiply_convert_fusion = bf16[128,2048]{1,0:T(8,128)(2,1)} fusion(bf16[128,4096]{1,0:T(8,128)(2,1)} %bitcast.12, bf16[128,4096]{1,0:T(8,128)(2,1)} %bitcast.10), kind=kLoop, calls=%fused_computation.2 | loop fusion | flops 1048576 | bytes 1572864 | tf_op jit(solution)/shard_map/convert_element_type | solution.py:325
  2.3 16.1 %collective-permute-start.7 = (bf16[128,2048]{1,0:T(8,128)(2,1)}, bf16[128,2048]{1,0:T(8,128)(2,1)S(1)}, u32[]{:S(2)}, u32[]{:S(2)}) collective-permute-start(bf16[128,2048]{1,0:T(8,128)(2,1)} %multiply_convert_fusion), channel_id=1, source_target_pairs={{0,7},{1,0},{2,1},{3,2},{4,3},{5,4},{6,5},{7,6},{8,15},{9,8},{10,9... | collective-permute-start | bytes 1572872 | tf_op jit(solution)/shard_map/ppermute | solution.py:273
  18.4 69.3 %conditional.2 = (bf16[128,2048]{1,0:T(8,128)(2,1)}, f32[2,10240]{1,0:T(2,128)}, f32[2,4096]{1,0:T(2,128)}, f32[2,4096]{1,0:T(2,128)}, f32[2,4096]{1,0:T(2,128)}...) conditional(s32[]{:T(128)} %convert_element_type.13, () %tuple.24, ...), branch_computations={%region_0.0_spmd, %region_1.0_spmd} | conditional | flops 7 | bytes 8323674 | solution.py:279
  18.4 5.6 %all_states.1 = f32[8,2,4096]{2,1,0:T(2,128)} custom-call(bf16[128,4096]{1,0:T(8,128)(2,1)S(1)} %get-tuple-element.34.refs_0_, bf16[128,4096]{1,0:T(8,128)(2,1)} %get-tuple-element.35.refs_1_, f32[16,4096]{1,0:T(8,128)S(1)} %bitcast.14), custom_call_target="tpu_custom_call" | custom-call | tf_op jit(solution)/shard_map/cond/branch_1_fun/all_states/pallas_call | solution.py:96
  24.0 4.6 %all-to-all-start.3 = ((f32[8,2,4096]{2,1,0:T(2,128)}), f32[8,2,4096]{2,1,0:T(2,128)S(1)}, u32[]{:S(2)}, u32[]{:S(2)}) async-start(f32[8,2,4096]{2,1,0:T(2,128)} %all_states.1), calls=%async_computation.3 | async-start | bytes 524288 | tf_op jit(solution)/shard_map/cond/branch_1_fun/all_to_all | solution.py:268
  29.3 6.9 %all-to-all-done.3.state_ref = f32[8,2,4096]{2,1,0:T(2,128)S(1)} async-done(((f32[8,2,4096]{2,1,0:T(2,128)}), f32[8,2,4096]{2,1,0:T(2,128)S(1)}, u32[]{:S(2)}, u32[]{:S(2)}) %all-to-all-start.3) | async-done | bytes 262176 | tf_op jit(solution)/shard_map/cond/branch_1_fun/all_to_all | solution.py:268
  36.9 1.7 %plane_sums.1 = (f32[2,4096]{1,0:T(2,128)}, f32[2,10240]{1,0:T(2,128)}, f32[8,2,2048]{2,1,0:T(2,128)}) custom-call(f32[8,2,4096]{2,1,0:T(2,128)} %copy-done.4, f32[2,4096]{1,0:T(2,128)} %get-tuple-element.86.rate_ref, f32[2,4096]{1,0:T(2,128)} %get-tuple-element.85.gain_ref), custom_call_target="tpu_custom_call" | custom-call | tf_op jit(solution)/shard_map/cond/branch_1_fun/plane_sums/pallas_call | solution.py:134
  38.6 2.4 %collective-permute-start = (f32[2,10240]{1,0:T(2,128)}, f32[2,10240]{1,0:T(2,128)}, u32[]{:S(2)}, u32[]{:S(2)}) collective-permute-start(f32[2,10240]{1,0:T(2,128)} %get-tuple-element.40), channel_id=1, source_target_pairs={{0,263},{1,256},{2,257},{3,258},{4,259},{5,260},{6,261},{7,262},{6... | collective-permute-start | bytes 245768 | tf_op jit(solution)/shard_map/cond/branch_1_fun/ppermute | solution.py:289
  41.0 3.4 %all-to-all-start.4 = ((f32[8,2,2048]{2,1,0:T(2,128)}), f32[8,2,2048]{2,1,0:T(2,128)S(1)}, u32[]{:S(2)}, u32[]{:S(2)}) async-start(f32[8,2,2048]{2,1,0:T(2,128)} %get-tuple-element.38), calls=%async_computation.4 | async-start | bytes 262144 | tf_op jit(solution)/shard_map/cond/branch_1_fun/all_to_all | solution.py:268
  45.7 8.5 %collective-permute-start.2 = (f32[2,4096]{1,0:T(2,128)S(1)}, f32[2,4096]{1,0:T(2,128)}, u32[]{:S(2)}, u32[]{:S(2)}) collective-permute-start(f32[2,4096]{1,0:T(2,128)S(1)} %copy-done.8), channel_id=1, source_target_pairs={{128,7},{129,0},{130,1},{131,2},{132,3},{133,4},{134,5},{135,6},{1... | collective-permute-start | bytes 98312 | tf_op jit(solution)/shard_map/cond/branch_1_fun/ppermute | solution.py:289
  54.2 1.9 %collective-permute-start.1 = (f32[2,4096]{1,0:T(2,128)S(1)}, f32[2,4096]{1,0:T(2,128)}, u32[]{:S(2)}, u32[]{:S(2)}) collective-permute-start(f32[2,4096]{1,0:T(2,128)S(1)} %copy-done.8), channel_id=1, source_target_pairs={{64,7},{65,0},{66,1},{67,2},{68,3},{69,4},{70,5},{71,6},{128,71},{... | collective-permute-start | bytes 98312 | tf_op jit(solution)/shard_map/cond/branch_1_fun/ppermute | solution.py:289
  56.2 5.0 %collective-permute-done.3 = f32[2,4096]{1,0:T(2,128)} collective-permute-done((f32[2,4096]{1,0:T(2,128)S(1)}, f32[2,4096]{1,0:T(2,128)}, u32[]{:S(2)}, u32[]{:S(2)}) %collective-permute-start.3) | collective-permute-done | bytes 32800 | tf_op jit(solution)/shard_map/cond/branch_1_fun/ppermute | solution.py:289
  61.2 7.7 %collective-permute-done.1 = f32[2,4096]{1,0:T(2,128)} collective-permute-done((f32[2,4096]{1,0:T(2,128)S(1)}, f32[2,4096]{1,0:T(2,128)}, u32[]{:S(2)}, u32[]{:S(2)}) %collective-permute-start.1) | collective-permute-done | bytes 32800 | tf_op jit(solution)/shard_map/cond/branch_1_fun/ppermute | solution.py:289
  68.8 6.6 %collective-permute-done = f32[2,10240]{1,0:T(2,128)} collective-permute-done((f32[2,10240]{1,0:T(2,128)}, f32[2,10240]{1,0:T(2,128)}, u32[]{:S(2)}, u32[]{:S(2)}) %collective-permute-start) | collective-permute-done | bytes 81952 | tf_op jit(solution)/shard_map/cond/branch_1_fun/ppermute | solution.py:289
  79.9 6.8 %sweep.2 = bf16[128,2048]{1,0:T(8,128)(2,1)} custom-call(bf16[128,4096]{1,0:T(8,128)(2,1)S(1)} %get-tuple-element.34.refs_0_, bf16[128,4096]{1,0:T(8,128)(2,1)S(1)} %copy-done.1, f32[8,2,2048]{2,1,0:T(2,128)} %copy-done.6, f32[16,4096]{1,0:T(8,128)S(1)} %bitcast.15, f32[16,4096]{1,0:T(8,128)S(1)} %bitcast.16), custom_call_target="tpu_custom_call" | custom-call | tf_op jit(solution)/shard_map/cond/branch_1_fun/sweep/pallas_call | solution.py:212
  87.7 21.3 %collective-permute-start.8 = (bf16[128,2048]{1,0:T(8,128)(2,1)}, bf16[128,2048]{1,0:T(8,128)(2,1)S(1)}, u32[]{:S(2)}, u32[]{:S(2)}) collective-permute-start(bf16[128,2048]{1,0:T(8,128)(2,1)} %get-tuple-element.78), channel_id=1, source_target_pairs={{0,7},{1,0},{2,1},{3,2},{4,3},{5,4},{6,5},{7,6},{8,15},{9,8},{10,9... | collective-permute-start | bytes 1572872 | tf_op jit(solution)/shard_map/ppermute | solution.py:273
  109.0 46.1 %conditional.3 = (bf16[128,4096]{1,0:T(8,128)(2,1)S(1)}, f32[8,2,4096]{2,1,0:T(2,128)}, f32[8,2,6144]{2,1,0:T(2,128)}) conditional(s32[]{:T(128)} %convert_element_type.13, () %tuple.23, (s32[]{:T(128)}, f32[2,10240]{1,0:T(2,128)}, bf16[128,2048]{1,0:T(8,128)(2,1)S(1)}, f32[2,4096]{1,0:T(2,128)}, f32[2,4096]{1,0:T(2,128)}, ...), branch_computations={%region_2.0_spmd, %region_3.0_spmd} | conditional | bytes 2113560 | solution.py:279
  109.9 12.3 %all_to_all.20.refs_1_.refs_2_.refs_3_ = f32[8,2,6144]{2,1,0:T(2,128)} all-to-all(f32[8,2,6144]{2,1,0:T(2,128)S(1)} %broadcast_in_dim.0), channel_id=1, replica_groups=mesh['plane'=8,'place'=8,'section'=8] {'place'}, dimensions={0} | all-to-all | bytes 786432 | tf_op jit(solution)/shard_map/cond/branch_1_fun/all_to_all | solution.py:268
  122.2 3.2 %early_states.1 = f32[8,2,2048]{2,1,0:T(2,128)} custom-call(bf16[128,2048]{1,0:T(8,128)(2,1)S(1)} %get-tuple-element.46.refs_0_, f32[8,2,6144]{2,1,0:T(2,128)} %all_to_all.20.refs_1_.refs_2_.refs_3_), custom_call_target="tpu_custom_call" | custom-call | tf_op jit(solution)/shard_map/cond/branch_1_fun/early_states/pallas_call | solution.py:108
  125.5 10.1 %all_to_all.21.state_ref = f32[8,2,2048]{2,1,0:T(2,128)} all-to-all(f32[8,2,2048]{2,1,0:T(2,128)} %early_states.1), channel_id=1, replica_groups=mesh['plane'=8,'place'=8,'section'=8] {'place'}, dimensions={0} | all-to-all | bytes 262144 | tf_op jit(solution)/shard_map/cond/branch_1_fun/all_to_all | solution.py:268
  135.6 1.7 %block_entries.1 = f32[8,2,4096]{2,1,0:T(2,128)} custom-call(s32[1]{0:T(128)} %bitcast.4.plane_ref, f32[8,2,2048]{2,1,0:T(2,128)} %all_to_all.21.state_ref, f32[2,10240]{1,0:T(2,128)} %get-tuple-element.48.full_ref, f32[2,4096]{1,0:T(2,128)} %get-tuple-element.49.refs_0_, f32[2,4096]{1,0:T(2,128)} %get-tuple-element.50.refs_1_, ...), custom_call_target="tpu_custom_call" | custom-call | tf_op jit(solution)/shard_map/cond/branch_1_fun/block_entries/pallas_call | solution.py:167
  137.3 11.6 %all_to_all.22.refs_1_ = f32[8,2,4096]{2,1,0:T(2,128)} all-to-all(f32[8,2,4096]{2,1,0:T(2,128)} %block_entries.1), channel_id=1, replica_groups=mesh['plane'=8,'place'=8,'section'=8] {'place'}, dimensions={0} | all-to-all | bytes 524288 | tf_op jit(solution)/shard_map/cond/branch_1_fun/all_to_all | solution.py:268
  148.9 6.2 %sweep.3 = bf16[128,4096]{1,0:T(8,128)(2,1)S(1)} custom-call(bf16[128,2048]{1,0:T(8,128)(2,1)S(1)} %get-tuple-element.46.refs_0_, f32[8,2,4096]{2,1,0:T(2,128)} %all_to_all.22.refs_1_, f32[8,2,6144]{2,1,0:T(2,128)} %all_to_all.20.refs_1_.refs_2_.refs_3_, f32[8,2,6144]{2,1,0:T(2,128)} %all_to_all.20.refs_1_.refs_2_.refs_3_), custom_call_target="tpu_custom_call" | custom-call | tf_op jit(solution)/shard_map/cond/branch_1_fun/sweep/pallas_call | solution.py:212
  156.2 3.3 %finish_late.1 = bf16[128,4096]{1,0:T(8,128)(2,1)} custom-call(bf16[128,4096]{1,0:T(8,128)(2,1)} %copy-done.2, bf16[128,2048]{1,0:T(8,128)(2,1)} %copy-done.5, f32[8,2,4096]{2,1,0:T(2,128)} %get-tuple-element.79.entry_ref, f32[8,2,6144]{2,1,0:T(2,128)} %get-tuple-element.80.decay_ref), custom_call_target="tpu_custom_call", output_to_operand_aliasing={{}: (0, {})} | custom-call | tf_op jit(solution)/shard_map/finish_late/pallas_call | solution.py:251
  (32 shorter events, 10.2 us)
Async XLA Ops:
  0.0 18.4 %copy-start = (bf16[1,128,4096]{2,1,0:T(8,128)(2,1)S(1)}, bf16[1,128,4096]{2,1,0:T(8,128)(2,1)}, u32[]{:S(2)}) copy-start(bf16[1,128,4096]{2,1,0:T(8,128)(2,1)} %param.8) | copy-start | bytes 3145732
  0.0 18.4 %copy-start.3 = (f32[1,16,4096]{2,1,0:T(8,128)S(1)}, f32[1,16,4096]{2,1,0:T(8,128)}, u32[]{:S(2)}) copy-start(f32[1,16,4096]{2,1,0:T(8,128)} %param.10) | copy-start | bytes 786436
  0.0 18.4 %copy-start.7 = (f32[1,16,4096]{2,1,0:T(8,128)S(1)}, f32[1,16,4096]{2,1,0:T(8,128)}, u32[]{:S(2)}) copy-start(f32[1,16,4096]{2,1,0:T(8,128)} %param.11) | copy-start | bytes 786436
  2.3 106.7 %collective-permute-start.7 = (bf16[128,2048]{1,0:T(8,128)(2,1)}, bf16[128,2048]{1,0:T(8,128)(2,1)S(1)}, u32[]{:S(2)}, u32[]{:S(2)}) collective-permute-start(bf16[128,2048]{1,0:T(8,128)(2,1)} %multiply_convert_fusion), channel_id=1, source_target_pairs={{0,7},{1,0},{2,1},{3,2},{4,3},{5,4},{6,5},{7,6},{8,15},{9,8},{10,9... | collective-permute-start | bytes 1572872 | tf_op jit(solution)/shard_map/ppermute | solution.py:273
  24.0 55.9 %copy-start.1 = (bf16[128,4096]{1,0:T(8,128)(2,1)S(1)}, bf16[128,4096]{1,0:T(8,128)(2,1)}, u32[]{:S(2)}) copy-start(bf16[128,4096]{1,0:T(8,128)(2,1)} %get-tuple-element.35.refs_1_) | copy-start | bytes 3145732 | tf_op jit(solution)/shard_map/cond
  24.0 12.1 %all-to-all-start.3 = ((f32[8,2,4096]{2,1,0:T(2,128)}), f32[8,2,4096]{2,1,0:T(2,128)S(1)}, u32[]{:S(2)}, u32[]{:S(2)}) async-start(f32[8,2,4096]{2,1,0:T(2,128)} %all_states.1), calls=%async_computation.3 | async-start | bytes 524288 | tf_op jit(solution)/shard_map/cond/branch_1_fun/all_to_all | solution.py:268
  36.2 0.7 copy-start.4
  38.6 36.9 %collective-permute-start = (f32[2,10240]{1,0:T(2,128)}, f32[2,10240]{1,0:T(2,128)}, u32[]{:S(2)}, u32[]{:S(2)}) collective-permute-start(f32[2,10240]{1,0:T(2,128)} %get-tuple-element.40), channel_id=1, source_target_pairs={{0,263},{1,256},{2,257},{3,258},{4,259},{5,260},{6,261},{7,262},{6... | collective-permute-start | bytes 245768 | tf_op jit(solution)/shard_map/cond/branch_1_fun/ppermute | solution.py:289
  41.0 3.4 %copy-start.8 = (f32[2,4096]{1,0:T(2,128)S(1)}, f32[2,4096]{1,0:T(2,128)}, u32[]{:S(2)}) copy-start(f32[2,4096]{1,0:T(2,128)} %get-tuple-element.45) | copy-start | bytes 98308 | tf_op jit(solution)/shard_map/cond
  41.0 38.2 %all-to-all-start.4 = ((f32[8,2,2048]{2,1,0:T(2,128)}), f32[8,2,2048]{2,1,0:T(2,128)S(1)}, u32[]{:S(2)}, u32[]{:S(2)}) async-start(f32[8,2,2048]{2,1,0:T(2,128)} %get-tuple-element.38), calls=%async_computation.4 | async-start | bytes 262144 | tf_op jit(solution)/shard_map/cond/branch_1_fun/all_to_all | solution.py:268
  44.4 16.7 %collective-permute-start.3 = (f32[2,4096]{1,0:T(2,128)S(1)}, f32[2,4096]{1,0:T(2,128)}, u32[]{:S(2)}, u32[]{:S(2)}) collective-permute-start(f32[2,4096]{1,0:T(2,128)S(1)} %copy-done.8), channel_id=1, source_target_pairs={{192,7},{193,0},{194,1},{195,2},{196,3},{197,4},{198,5},{199,6},{2... | collective-permute-start | bytes 98312 | tf_op jit(solution)/shard_map/cond/branch_1_fun/ppermute | solution.py:289
  45.7 15.4 %collective-permute-start.2 = (f32[2,4096]{1,0:T(2,128)S(1)}, f32[2,4096]{1,0:T(2,128)}, u32[]{:S(2)}, u32[]{:S(2)}) collective-permute-start(f32[2,4096]{1,0:T(2,128)S(1)} %copy-done.8), channel_id=1, source_target_pairs={{128,7},{129,0},{130,1},{131,2},{132,3},{133,4},{134,5},{135,6},{1... | collective-permute-start | bytes 98312 | tf_op jit(solution)/shard_map/cond/branch_1_fun/ppermute | solution.py:289
  54.2 14.6 %collective-permute-start.1 = (f32[2,4096]{1,0:T(2,128)S(1)}, f32[2,4096]{1,0:T(2,128)}, u32[]{:S(2)}, u32[]{:S(2)}) collective-permute-start(f32[2,4096]{1,0:T(2,128)S(1)} %copy-done.8), channel_id=1, source_target_pairs={{64,7},{65,0},{66,1},{67,2},{68,3},{69,4},{70,5},{71,6},{128,71},{... | collective-permute-start | bytes 98312 | tf_op jit(solution)/shard_map/cond/branch_1_fun/ppermute | solution.py:289
  75.4 11.3 %collective-permute-start.6 = (f32[2,4096]{1,0:T(2,128)S(1)}, f32[2,4096]{1,0:T(2,128)}, u32[]{:S(2)}, u32[]{:S(2)}) collective-permute-start(f32[2,4096]{1,0:T(2,128)S(1)} %copy-done.8), channel_id=1, source_target_pairs={{448,7},{449,0},{450,1},{451,2},{452,3},{453,4},{454,5},{455,6},{4... | collective-permute-start | bytes 98312 | tf_op jit(solution)/shard_map/cond/branch_1_fun/ppermute | solution.py:289
  76.7 10.0 %collective-permute-start.5 = (f32[2,4096]{1,0:T(2,128)S(1)}, f32[2,4096]{1,0:T(2,128)}, u32[]{:S(2)}, u32[]{:S(2)}) collective-permute-start(f32[2,4096]{1,0:T(2,128)S(1)} %copy-done.8), channel_id=1, source_target_pairs={{384,7},{385,0},{386,1},{387,2},{388,3},{389,4},{390,5},{391,6},{4... | collective-permute-start | bytes 98312 | tf_op jit(solution)/shard_map/cond/branch_1_fun/ppermute | solution.py:289
  78.0 9.7 %collective-permute-start.4 = (f32[2,4096]{1,0:T(2,128)S(1)}, f32[2,4096]{1,0:T(2,128)}, u32[]{:S(2)}, u32[]{:S(2)}) collective-permute-start(f32[2,4096]{1,0:T(2,128)S(1)} %copy-done.8), channel_id=1, source_target_pairs={{320,7},{321,0},{322,1},{323,2},{324,3},{325,4},{326,5},{327,6},{3... | collective-permute-start | bytes 98312 | tf_op jit(solution)/shard_map/cond/branch_1_fun/ppermute | solution.py:289
  79.3 0.7 copy-start.6
  87.7 67.4 %collective-permute-start.8 = (bf16[128,2048]{1,0:T(8,128)(2,1)}, bf16[128,2048]{1,0:T(8,128)(2,1)S(1)}, u32[]{:S(2)}, u32[]{:S(2)}) collective-permute-start(bf16[128,2048]{1,0:T(8,128)(2,1)} %get-tuple-element.78), channel_id=1, source_target_pairs={{0,7},{1,0},{2,1},{3,2},{4,3},{5,4},{6,5},{7,6},{8,15},{9,8},{10,9... | collective-permute-start | bytes 1572872 | tf_op jit(solution)/shard_map/ppermute | solution.py:273
  155.1 1.0 copy-start.2
  155.1 1.1 copy-start.5

commit v3 on v2

--- a/solution.py
+++ b/solution.py
@@ -29,6 +29,15 @@
 def mode_row(ref, j, lanes):
     row = ref[j : j + 1, lanes] if len(ref.shape) == 2 else ref[j // SLOT, j % SLOT : j % SLOT + 1, lanes]
     return jnp.broadcast_to(row, (8, 128))
+
+
+def outer_rows(ref, lanes):
+    parts = ref[:, :, lanes].astype(F32)
+    chips = [parts[2 * c] + parts[2 * c + 1] for c in range(PLACES // 2)]
+    return [
+        jnp.broadcast_to(chips[j // (2 * SLOT)][j % (2 * SLOT)][None], (8, 128))
+        for j in range(MODES)
+    ]
 
 
 def source_rows(refs, rows, lanes):
@@ -115,61 +124,66 @@
     )(*parts, decay)
 
 
-def plane_kernel(state_ref, rate_ref, gain_ref, sum_ref, full_ref, entry_ref):
-    channels = rate_ref.shape[1]
+def plane_kernel(state_ref, rate_ref, gain_ref, out_ref):
+    late = rate_ref.shape[1] - EARLY
     step = jnp.exp(-float(ROWS) * rate_ref[...])
     total = jnp.zeros_like(step)
     for k in reversed(range(PLACES)):
-        entry_ref[k] = total[:, EARLY:]
+        out_ref[k, :, :late] = total[:, EARLY:]
         total = total * step + state_ref[k]
-    for ref in (sum_ref, full_ref):
-        ref[:, :EARLY] = total[:, :EARLY]
-        ref[:, EARLY:channels] = total[:, EARLY:] * gain_ref[:, EARLY:]
-    full_ref[:, channels : 2 * channels] = rate_ref[...]
-    full_ref[:, 2 * channels :] = gain_ref[:, :EARLY]
+    total = total * gain_ref[...]
+    for k in range(PLACES):
+        out_ref[k, :, late:] = total
 
 
 def plane_sums(states, rates, gains):
     channels = rates.shape[1]
     return pl.pallas_call(
         plane_kernel,
-        out_shape=[
-            jax.ShapeDtypeStruct((SLOT, channels), F32),
-            jax.ShapeDtypeStruct((SLOT, 2 * channels + EARLY), F32),
-            jax.ShapeDtypeStruct((PLACES, SLOT, channels - EARLY), F32),
-        ],
+        out_shape=jax.ShapeDtypeStruct((PLACES, SLOT, 2 * channels - EARLY), F32),
         name="plane_sums",
     )(states, rates, gains)
 
 
-def entry_kernel(plane_ref, state_ref, full_ref, *refs):
+def inner_kernel(state_ref, param_ref, entry_ref):
+    step = jnp.exp(-float(ROWS) * param_ref[:, :EARLY])
+    total = jnp.zeros_like(step)
+    for k in reversed(range(PLACES)):
+        entry_ref[k] = total
+        total = total * step + state_ref[k]
+
+
+def inner_entries(states, params):
+    return pl.pallas_call(
+        inner_kernel,
+        out_shape=jax.ShapeDtypeStruct(states.shape, F32),
+        name="inner_entries",
+    )(states, params)
+
+
+def outer_kernel(core_ref, rate_ref, *refs):
     sum_refs, entry_ref = refs[:-1], refs[-1]
-    channels = entry_ref.shape[2]
-    rates = full_ref[:, channels : 2 * channels]
+    rates = rate_ref[...]
     stride = jnp.exp(-float(ROWS * PLACES) * rates)
-    middle = jnp.where(plane_ref[0] < PLANES - HALF, full_ref[:, :channels], 0.0)
-    values = [ref[...] for ref in sum_refs]
-    values.insert(HALF - 1, middle)
-    carry = values.pop()
-    while values:
-        carry = carry * stride + values.pop()
+    carry = sum_refs[-1][...].astype(F32)
+    for sum_ref in sum_refs[-2::-1]:
+        carry = carry * stride + sum_ref[...].astype(F32)
+    beyond = jnp.exp(-float(ROWS * PLACES * HALF) * rates)
+    carry = jnp.where(core_ref[0] == 0, carry, carry * beyond)
     step = jnp.exp(-float(ROWS) * rates)
-    early, late = carry[:, :EARLY], carry[:, EARLY:]
     for k in reversed(range(PLACES)):
-        entry_ref[k, :, :EARLY] = early
-        entry_ref[k, :, EARLY:] = late
-        early = early * step[:, :EARLY] + state_ref[k]
-        late = late * step[:, EARLY:]
-
-
-def block_entries(plane, states, full, sums):
+        entry_ref[k] = carry.astype(jnp.bfloat16)
+        carry = carry * step
+
+
+def outer_entries(core, rates, sums):
     whole = pl.BlockSpec(memory_space=pltpu.VMEM)
     return pl.pallas_call(
-        entry_kernel,
-        in_specs=[pl.BlockSpec(memory_space=pltpu.SMEM)] + [whole] * (2 + len(sums)),
-        out_shape=jax.ShapeDtypeStruct((PLACES, SLOT, sums[0].shape[1]), F32),
-        name="block_entries",
-    )(plane, states, full, *sums)
+        outer_kernel,
+        in_specs=[pl.BlockSpec(memory_space=pltpu.SMEM)] + [whole] * (1 + len(sums)),
+        out_shape=jax.ShapeDtypeStruct((PLACES,) + rates.shape, jnp.bfloat16),
+        name="outer_entries",
+    )(core, rates, *sums)
 
 
 def sweep_kernel(sources, entry_ref, decay_ref, gain_ref, out_ref, source, result):
@@ -208,28 +222,27 @@
     lax.fori_loop(0, WIDTH // 128, one_group, 0)
 
 
-def sweep(sources, specs, counts, params, channels, out_channels):
+def sweep(sources, specs, counts, params, channels):
     return pl.pallas_call(
         in_parts(sweep_kernel, len(sources), counts),
         grid=(channels // WIDTH,),
         in_specs=specs + [columns(a.shape, first) for a, first in params],
-        out_specs=columns((ROWS, out_channels)),
-        out_shape=jax.ShapeDtypeStruct((ROWS, out_channels), jnp.bfloat16),
+        out_specs=columns((ROWS, channels)),
+        out_shape=jax.ShapeDtypeStruct((ROWS, channels), jnp.bfloat16),
         scratch_shapes=[pltpu.VMEM((ROWS, 128), F32), pltpu.VMEM((ROWS, 128), F32)],
         name="sweep",
     )(*sources, *(a for a, _ in params))
 
 
-def finish_kernel(_, late_ref, entry_ref, decay_ref, out_ref):
+def finish_kernel(sources, entry_ref, decay_ref, out_ref):
     ahead = 8.0 - lax.broadcasted_iota(jnp.int32, (8, 128), 0).astype(F32)
 
     def one_group(group, _):
         lanes = lanes_of(group)
         rates = [mode_row(decay_ref, j, lanes) for j in range(MODES)]
         leap = [jnp.exp(-8.0 * r) for r in rates]
-        held = [
-            mode_row(entry_ref, j, lanes) * jnp.exp(-r * ahead) for j, r in enumerate(rates)
-        ]
+        enter = outer_rows(entry_ref, lanes)
+        held = [e * jnp.exp(-r * ahead) for e, r in zip(enter, rates)]
         for pair in reversed(range(ROWS // 16)):
             rows = slice(16 * pair, 16 * pair + 16)
             halves = []
@@ -240,28 +253,23 @@
                 halves.append(terms[0])
                 held = [h * q for h, q in zip(held, leap)]
             whole = jnp.concatenate(halves[::-1], axis=0)
-            out_ref[rows, lanes] = (late_ref[rows, lanes].astype(F32) + whole).astype(jnp.bfloat16)
+            out_ref[rows, lanes] = (source_rows(sources, rows, lanes) + whole).astype(jnp.bfloat16)
         return 0
 
     lax.fori_loop(0, WIDTH // 128, one_group, 0)
 
 
-def finish_late(out, late_rows, entries, decay):
-    late = late_rows.shape[1]
-    return pl.pallas_call(
-        finish_kernel,
-        grid=(late // WIDTH,),
-        in_specs=[
-            pl.BlockSpec(memory_space=pl.ANY),
-            columns(late_rows.shape),
-            columns(entries.shape, EARLY),
-            columns(decay.shape, EARLY),
-        ],
-        out_specs=columns(out.shape, EARLY),
-        out_shape=pltpu.HBM(out.shape, out.dtype),
-        input_output_aliases={0: 0},
-        name="finish_late",
-    )(out, late_rows, entries, decay)
+def finish(parts, entries, decay):
+    specs, counts = part_columns(parts)
+    channels = entries.shape[2]
+    return pl.pallas_call(
+        in_parts(finish_kernel, len(parts), counts),
+        grid=(sum(counts),),
+        in_specs=specs + [columns(entries.shape), columns((PLACES, SLOT, channels))],
+        out_specs=columns((ROWS, channels)),
+        out_shape=pltpu.HBM((ROWS, channels), jnp.bfloat16),
+        name="finish",
+    )(*parts, entries, decay)
 
 
 def exchange(values, axis):
@@ -279,56 +287,78 @@
     return lax.cond(always, step, empty, *args)
 
 
-def from_plane(message, by, ring):
+def half_ring(message):
     planes, sections = lax.axis_size("plane"), lax.axis_size("section")
     pairs = [
-        (z * sections + s, (z - by) % planes * sections + (s - 1) % sections)
-        for z in range(0 if ring else by, planes)
+        (z * sections + s, (z + HALF) % planes * sections + (s - 1) % sections)
+        for z in range(planes)
         for s in range(sections)
     ]
     return lax.ppermute(message, ("plane", "section"), pairs)
 
 
-def late_step(gate, grad, decay, gain):
-    late = gate.shape[1] - EARLY
-    first = SLOT * lax.axis_index("place")
-    rates = lax.dynamic_slice_in_dim(decay, first, SLOT, axis=0)
-    gains = lax.dynamic_slice_in_dim(gain, first, SLOT, axis=0)
+def from_later(sums, near):
+    sections = lax.axis_size("section")
+    number = lambda z, k, s: (z * PLACES + k) * sections + s % sections
+    pairs = [
+        (number(z, k, s), number(z - near - k % 2 * HALF, k, s - 1))
+        for k in range(PLACES)
+        for z in range(near + k % 2 * HALF, PLANES)
+        for s in range(sections)
+    ]
+    return lax.ppermute(sums, ("plane", "place", "section"), pairs)
+
+
+def late_step(gate, grad, decay, gain, rates, gains):
+    channels = gate.shape[1]
+    late = channels - EARLY
     states = exchange(all_states(gate, grad, decay), "place")
-    total, full, entries = plane_sums(states, rates, gains)
-    full = from_plane(full, HALF, True)
-    sums = [from_plane(total, k, False) for k in range(1, HALF)]
-    total, full, *sums = lax.optimization_barrier((total, full, *sums))
-    sums += [from_plane(total, k, False) for k in range(HALF + 1, PLANES)]
-    entries = exchange(entries, "place")
+    spread = exchange(plane_sums(states, rates, gains), "place")
+    chip = lax.axis_index("place") // 2 * 2
+    sums = lax.dynamic_slice(spread, (chip, 0, late), (2, SLOT, channels))
+    sums = sums.reshape(2 * SLOT, channels).astype(jnp.bfloat16)
     sources = [gate, grad]
     specs = [columns(s.shape, EARLY) for s in sources]
-    params = [(entries, 0), (decay, EARLY), (gain, EARLY)]
-    return sweep(sources, specs, [1], params, late, late), full, sums
-
-
-def early_step(plane, gated, full, sums):
-    channels = sums[0].shape[1]
+    inputs = [(spread, 0), (decay, EARLY), (gain, EARLY)]
+    return sweep(sources, specs, [1], inputs, late), sums
+
+
+def early_step(gated, params, sums):
     specs, counts = part_columns([gated])
-    params = jnp.broadcast_to(full[None, :, channels:], (PLACES, SLOT, channels + EARLY))
-    params = exchange(params, "place")
-    states = exchange(early_states([gated], params, 0), "place")
-    entries = exchange(block_entries(plane, states, full, sums), "place")
-    columns_of = [(entries, 0), (params, 0), (params, channels)]
-    return sweep([gated], specs, counts, columns_of, EARLY, channels), entries, params
+    channels = params.shape[1] - EARLY
+    sums = [from_later(sums, k) for k in range(1, HALF + 1)]
+    everywhere = exchange(jnp.broadcast_to(params[None], (PLACES,) + params.shape), "place")
+    states = exchange(early_states([gated], everywhere, 0), "place")
+    entries = exchange(inner_entries(states, params), "place")
+    inputs = [(entries, 0), (everywhere, 0), (everywhere, channels)]
+    chip = lax.axis_index("place") // 2 * 2
+    rates = lax.dynamic_slice(everywhere, (chip, 0, 0), (2, SLOT, channels))
+    rates = rates.reshape(2 * SLOT, channels)
+    return sweep([gated], specs, counts, inputs, EARLY), everywhere, rates, sums
+
+
+def last_step(core, rates, sums):
+    return exchange(outer_entries(core, rates, sums), "place")
 
 
 def shards(gate, grad, decay, amplitude):
     gate, grad, decay, gain = gate[0], grad[0], decay[0], amplitude[0]
-    always = lax.axis_index("place") >= 0
-    plane = lax.axis_index("plane").reshape(1)
+    place = lax.axis_index("place")
+    always = place >= 0
+    core = (place % 2).reshape(1)
+    rates = lax.dynamic_slice_in_dim(decay, SLOT * place, SLOT, axis=0)
+    gains = lax.dynamic_slice_in_dim(gain, SLOT * place, SLOT, axis=0)
+    params = half_ring(jnp.concatenate([rates, gains[:, :EARLY]], axis=1))
     gated = (gate[:, :EARLY].astype(F32) * grad[:, :EARLY].astype(F32)).astype(jnp.bfloat16)
     arrived = passed_along(gated, "section", -1)
-    gate, grad, gated = lax.optimization_barrier((gate, grad, gated))
-    local, full, sums = as_one_step(always, late_step, gate, grad, decay, gain)
+    gate, grad, gated, params = lax.optimization_barrier((gate, grad, gated, params))
+    local, sums = as_one_step(always, late_step, gate, grad, decay, gain, rates, gains)
     late_rows = passed_along(local, "section", -1)
-    out, entries, params = as_one_step(always, early_step, plane, arrived, full, sums)
-    return finish_late(out, late_rows, entries, params)[None]
+    early_rows, everywhere, rates, sums = as_one_step(
+        always, early_step, arrived, params, sums
+    )
+    entries = as_one_step(always, last_step, core, rates, sums)
+    return finish([early_rows, late_rows], entries, everywhere)[None]
 
 
 def solution(mesh):

time: 161 us -> 149 us (0.925)
  the two profiles are of different devices: /device:TPU:64 before, /device:TPU:192 now
where the time goes in v3:
time: 149 us; the launch traced here: 148 us
  starting transfers between devices  54.3 us (36%)
  blocking collectives  37 us (25%)
  Pallas kernels  32 us (21%)
  waiting for transfers between devices  14.1 us (9%)
  local copies, waits for them, and re-layouts  7.71 us (5%)
  other arithmetic  2.2 us (1%)
    all_to_all x3, blocking collectives, exchange(): return lax.all_to_all(values, axis, split_axis=0, concat_axis=0, tiled=True)  37 us
    ppermute x4, starting transfers between devices, from_later(): return lax.ppermute(sums, ('plane', 'place', 'section'), pairs)  18.3 us
    ppermute x2, starting transfers between devices, passed_along(): lax.ppermute(shard, axis, [(i, (i + by) % count) for i in range(count)])  14.8 us
    all_to_all x3, waiting for transfers between devices, exchange(): return lax.all_to_all(values, axis, split_axis=0, concat_axis=0, tiled=True)  14.1 us
    pallas_call x2, Pallas kernels, sweep(): pl.pallas_call(in_parts(sweep_kernel, len(sources), counts), grid=(channe...  13 us
    all_to_all x3, starting transfers between devices, exchange(): return lax.all_to_all(values, axis, split_axis=0, concat_axis=0, tiled=True)  11.7 us
    ppermute x1, starting transfers between devices, half_ring(): return lax.ppermute(message, ('plane', 'section'), pairs)  9.49 us
    pallas_call x1, Pallas kernels, all_states(): pl.pallas_call(in_parts(state_kernel, 2, [1]), grid=(channels // width,),...  5.58 us
  transfers between devices with their start and end apart: 10, of which 2 were waited for; matrix products, arithmetic and copies ran while one was open for 4% of the time, Pallas kernels for 18%

profile of v3, /device:TPU:192, one launch (start us, length us, event | category | flops | bytes accessed | tf_op | source)
XLA Modules:
  0.0 147.5 jit_solution(16472125995659119188)
XLA Ops:
  1.1 9.5 %collective-permute-start.4 = (f32[2,6144]{1,0:T(2,128)S(1)}, f32[2,6144]{1,0:T(2,128)S(1)}, u32[]{:S(2)}, u32[]{:S(2)}) collective-permute-start(f32[2,6144]{1,0:T(2,128)S(1)} %pad_maximum_fusion), channel_id=1, source_target_pairs={{0,263},{1,256},{2,257},{3,258},{4,259},{5,260},{6,261},{7,262},{6... | collective-permute-start | bytes 147464 | tf_op jit(solution)/shard_map/ppermute | solution.py:297
  10.7 2.2 %multiply_convert_fusion = bf16[128,2048]{1,0:T(8,128)(2,1)} fusion(bf16[128,4096]{1,0:T(8,128)(2,1)} %bitcast.10, bf16[128,4096]{1,0:T(8,128)(2,1)} %bitcast.12), kind=kLoop, calls=%fused_computation.2 | loop fusion | flops 1048576 | bytes 1572864 | tf_op jit(solution)/shard_map/convert_element_type | solution.py:352
  12.8 3.7 %collective-permute-start.5 = (bf16[128,2048]{1,0:T(8,128)(2,1)}, bf16[128,2048]{1,0:T(8,128)(2,1)S(1)}, u32[]{:S(2)}, u32[]{:S(2)}) collective-permute-start(bf16[128,2048]{1,0:T(8,128)(2,1)} %multiply_convert_fusion), channel_id=1, source_target_pairs={{0,7},{1,0},{2,1},{3,2},{4,3},{5,4},{6,5},{7,6},{8,15},{9,8},{10,9... | collective-permute-start | bytes 1572872 | tf_op jit(solution)/shard_map/ppermute | solution.py:281
  17.2 40.8 %conditional.3 = (bf16[128,2048]{1,0:T(8,128)(2,1)}, bf16[4,4096]{1,0:T(4,128)(2,1)}) conditional(s32[]{:T(128)} %convert_element_type.20, () %tuple.33, (f32[1,16,4096]{2,1,0:T(8,128)S(1)}, bf16[128,4096]{1,0:T(8,128)(2,1)}, bf16[128,4096]{1,0:T(8,128)(2,1)S(1)}, f32[2,4096]{1,0:T(2,128)S(1)}, f32[2,4096]{1,0:T(2,128)S(1)}, ...), branch_computations={%region_0.1_spmd, %region_1.2_spmd} | conditional | flops 22 | bytes 7602512 | solution.py:287
  17.2 5.6 %all_states.1 = f32[8,2,4096]{2,1,0:T(2,128)} custom-call(bf16[128,4096]{1,0:T(8,128)(2,1)} %get-tuple-element.64.refs_0_, bf16[128,4096]{1,0:T(8,128)(2,1)S(1)} %get-tuple-element.65.refs_1_, f32[16,4096]{1,0:T(8,128)S(1)} %bitcast.14), custom_call_target="tpu_custom_call" | custom-call | tf_op jit(solution)/shard_map/cond/branch_1_fun/all_states/pallas_call | solution.py:105
  22.8 12.2 %all_to_all.24.state_ref = f32[8,2,4096]{2,1,0:T(2,128)} all-to-all(f32[8,2,4096]{2,1,0:T(2,128)} %all_states.1), channel_id=1, replica_groups=mesh['plane'=8,'place'=8,'section'=8] {'place'}, dimensions={0} | all-to-all | bytes 524288 | tf_op jit(solution)/shard_map/cond/branch_1_fun/all_to_all | solution.py:276
  36.8 3.5 %all-to-all-start.2 = ((f32[8,2,6144]{2,1,0:T(2,128)}), f32[8,2,6144]{2,1,0:T(2,128)S(1)}, u32[]{:S(2)}, u32[]{:S(2)}) async-start(f32[8,2,6144]{2,1,0:T(2,128)} %plane_sums.1), calls=%async_computation.2 | async-start | bytes 786432 | tf_op jit(solution)/shard_map/cond/branch_1_fun/all_to_all | solution.py:276
  40.3 8.8 %all-to-all-done.2.refs_2_ = f32[8,2,6144]{2,1,0:T(2,128)S(1)} async-done(((f32[8,2,6144]{2,1,0:T(2,128)}), f32[8,2,6144]{2,1,0:T(2,128)S(1)}, u32[]{:S(2)}, u32[]{:S(2)}) %all-to-all-start.2) | async-done | bytes 393248 | tf_op jit(solution)/shard_map/cond/branch_1_fun/all_to_all | solution.py:276
  51.2 6.8 %sweep.2 = bf16[128,2048]{1,0:T(8,128)(2,1)} custom-call(bf16[128,4096]{1,0:T(8,128)(2,1)S(1)} %copy-done.1, bf16[128,4096]{1,0:T(8,128)(2,1)S(1)} %get-tuple-element.65.refs_1_, f32[8,2,6144]{2,1,0:T(2,128)} %copy-done.2, f32[16,4096]{1,0:T(8,128)S(1)} %bitcast.15, f32[16,4096]{1,0:T(8,128)S(1)} %bitcast.16), custom_call_target="tpu_custom_call" | custom-call | tf_op jit(solution)/shard_map/cond/branch_1_fun/sweep/pallas_call | solution.py:226
  58.0 11.1 %collective-permute-start.6 = (bf16[128,2048]{1,0:T(8,128)(2,1)}, bf16[128,2048]{1,0:T(8,128)(2,1)S(1)}, u32[]{:S(2)}, u32[]{:S(2)}) collective-permute-start(bf16[128,2048]{1,0:T(8,128)(2,1)} %get-tuple-element.96), channel_id=1, source_target_pairs={{0,7},{1,0},{2,1},{3,2},{4,3},{5,4},{6,5},{7,6},{8,15},{9,8},{10,9... | collective-permute-start | bytes 1572872 | tf_op jit(solution)/shard_map/ppermute | solution.py:281
  69.1 59.9 %conditional.4 = (bf16[128,2048]{1,0:T(8,128)(2,1)S(1)}, f32[8,2,6144]{2,1,0:T(2,128)}, f32[4,4096]{1,0:T(4,128)S(1)}, bf16[4,4096]{1,0:T(4,128)(2,1)}, bf16[4,4...) conditional(s32[]{:T(128)} %convert_element_type.20, () %tuple.31, (f32[2,6144]{1,0:T(2,128)}, ...), branch_computations={%region_2.3_spmd, %region_3.4_spmd} | conditional | flops 22 | bytes 4047444 | solution.py:287
  70.0 13.9 %all_to_all.25.refs_1_.refs_2_.refs_3_ = f32[8,2,6144]{2,1,0:T(2,128)} all-to-all(f32[8,2,6144]{2,1,0:T(2,128)S(1)} %broadcast_in_dim.0), channel_id=1, replica_groups=mesh['plane'=8,'place'=8,'section'=8] {'place'}, dimensions={0} | all-to-all | bytes 786432 | tf_op jit(solution)/shard_map/cond/branch_1_fun/all_to_all | solution.py:276
  83.9 3.2 %early_states.1 = f32[8,2,2048]{2,1,0:T(2,128)} custom-call(bf16[128,2048]{1,0:T(8,128)(2,1)S(1)} %get-tuple-element.70.refs_0_, f32[8,2,6144]{2,1,0:T(2,128)} %all_to_all.25.refs_1_.refs_2_.refs_3_), custom_call_target="tpu_custom_call" | custom-call | tf_op jit(solution)/shard_map/cond/branch_1_fun/early_states/pallas_call | solution.py:117
  87.2 3.5 %all-to-all-start.4 = ((f32[8,2,2048]{2,1,0:T(2,128)}), f32[8,2,2048]{2,1,0:T(2,128)S(1)}, u32[]{:S(2)}, u32[]{:S(2)}) async-start(f32[8,2,2048]{2,1,0:T(2,128)} %early_states.1), calls=%async_computation.4 | async-start | bytes 262144 | tf_op jit(solution)/shard_map/cond/branch_1_fun/all_to_all | solution.py:276
  90.7 4.3 %collective-permute-start.3 = (bf16[4,4096]{1,0:T(4,128)(2,1)}, bf16[4,4096]{1,0:T(4,128)(2,1)}, u32[]{:S(2)}, u32[]{:S(2)}) collective-permute-start(bf16[4,4096]{1,0:T(4,128)(2,1)} %get-tuple-element.72), channel_id=1, source_target_pairs={{256,7},{257,0},{258,1},{259,2},{260,3},{261,4},{262,5},{263,6},{3... | collective-permute-start | bytes 98312 | tf_op jit(solution)/shard_map/cond/branch_1_fun/ppermute | solution.py:309
  95.0 4.8 %collective-permute-start.2 = (bf16[4,4096]{1,0:T(4,128)(2,1)}, bf16[4,4096]{1,0:T(4,128)(2,1)}, u32[]{:S(2)}, u32[]{:S(2)}) collective-permute-start(bf16[4,4096]{1,0:T(4,128)(2,1)} %get-tuple-element.72), channel_id=1, source_target_pairs={{192,7},{193,0},{194,1},{195,2},{196,3},{197,4},{198,5},{199,6},{2... | collective-permute-start | bytes 98312 | tf_op jit(solution)/shard_map/cond/branch_1_fun/ppermute | solution.py:309
  99.8 2.8 %collective-permute-start.1 = (bf16[4,4096]{1,0:T(4,128)(2,1)}, bf16[4,4096]{1,0:T(4,128)(2,1)}, u32[]{:S(2)}, u32[]{:S(2)}) collective-permute-start(bf16[4,4096]{1,0:T(4,128)(2,1)} %get-tuple-element.72), channel_id=1, source_target_pairs={{128,7},{129,0},{130,1},{131,2},{132,3},{133,4},{134,5},{135,6},{1... | collective-permute-start | bytes 98312 | tf_op jit(solution)/shard_map/cond/branch_1_fun/ppermute | solution.py:309
  102.5 6.4 %collective-permute-start = (bf16[4,4096]{1,0:T(4,128)(2,1)}, bf16[4,4096]{1,0:T(4,128)(2,1)}, u32[]{:S(2)}, u32[]{:S(2)}) collective-permute-start(bf16[4,4096]{1,0:T(4,128)(2,1)} %get-tuple-element.72), channel_id=1, source_target_pairs={{64,7},{65,0},{66,1},{67,2},{68,3},{69,4},{70,5},{71,6},{128,71},{... | collective-permute-start | bytes 98312 | tf_op jit(solution)/shard_map/cond/branch_1_fun/ppermute | solution.py:309
  111.3 4.7 %all-to-all-start.5 = ((f32[8,2,2048]{2,1,0:T(2,128)}), f32[8,2,2048]{2,1,0:T(2,128)S(1)}, u32[]{:S(2)}, u32[]{:S(2)}) async-start(f32[8,2,2048]{2,1,0:T(2,128)} %inner_entries.1), calls=%async_computation.5 | async-start | bytes 262144 | tf_op jit(solution)/shard_map/cond/branch_1_fun/all_to_all | solution.py:276
  116.9 5.2 %all-to-all-done.5.refs_1_ = f32[8,2,2048]{2,1,0:T(2,128)S(1)} async-done(((f32[8,2,2048]{2,1,0:T(2,128)}), f32[8,2,2048]{2,1,0:T(2,128)S(1)}, u32[]{:S(2)}, u32[]{:S(2)}) %all-to-all-start.5) | async-done | bytes 131104 | tf_op jit(solution)/shard_map/cond/branch_1_fun/all_to_all | solution.py:276
  122.8 6.2 %sweep.3 = bf16[128,2048]{1,0:T(8,128)(2,1)S(1)} custom-call(bf16[128,2048]{1,0:T(8,128)(2,1)S(1)} %get-tuple-element.70.refs_0_, f32[8,2,2048]{2,1,0:T(2,128)} %copy-done.6, f32[8,2,6144]{2,1,0:T(2,128)} %all_to_all.25.refs_1_.refs_2_.refs_3_, f32[8,2,6144]{2,1,0:T(2,128)} %all_to_all.25.refs_1_.refs_2_.refs_3_), custom_call_target="tpu_custom_call" | custom-call | tf_op jit(solution)/shard_map/cond/branch_1_fun/sweep/pallas_call | solution.py:226
  129.0 12.5 %conditional.5 = (bf16[8,4,4096]{2,1,0:T(4,128)(2,1)S(1)}) conditional(s32[]{:T(128)} %convert_element_type.20, () %tuple.36, (s32[]{:T(128)}, f32[4,4096]{1,0:T(4,128)S(1)}, bf16[4,4096]{1,0:T(4,128)(2,1)}, bf16[4,4096]{1,0:T(4,128)(2,1)}, bf16[4,4096]{1,0:T(4,128)(2,1)}, /*index=5*/bf16[4,4096]{1,0:T(4,128)(2,1)}) %tuple.37), branch_computations={%region_4.5_spmd, %region_5.6_spmd} | conditional | flops 11 | bytes 524405 | solution.py:287
  130.7 10.8 %all_to_all.26 = bf16[8,4,4096]{2,1,0:T(4,128)(2,1)S(1)} all-to-all(bf16[8,4,4096]{2,1,0:T(4,128)(2,1)} %outer_entries.1), channel_id=1, replica_groups=mesh['plane'=8,'place'=8,'section'=8] {'place'}, dimensions={0} | all-to-all | bytes 524288 | tf_op jit(solution)/shard_map/cond/branch_1_fun/all_to_all | solution.py:276
  142.3 5.2 %finish.1 = bf16[128,4096]{1,0:T(8,128)(2,1)} custom-call(bf16[128,2048]{1,0:T(8,128)(2,1)S(1)} %get-tuple-element.95.refs_0_, bf16[128,2048]{1,0:T(8,128)(2,1)} %copy-done.5, bf16[8,4,4096]{2,1,0:T(4,128)(2,1)S(1)} %get-tuple-element.123.refs_2_, f32[8,2,6144]{2,1,0:T(2,128)} %get-tuple-element.102.refs_3_), custom_call_target="tpu_custom_call" | custom-call | tf_op jit(solution)/shard_map/finish/pallas_call | solution.py:265
  (39 shorter events, 12.7 us)
Async XLA Ops:
  0.0 16.6 %copy-start = (bf16[1,128,4096]{2,1,0:T(8,128)(2,1)S(1)}, bf16[1,128,4096]{2,1,0:T(8,128)(2,1)}, u32[]{:S(2)}) copy-start(bf16[1,128,4096]{2,1,0:T(8,128)(2,1)} %param.11) | copy-start | bytes 3145732
  1.1 15.4 %collective-permute-start.4 = (f32[2,6144]{1,0:T(2,128)S(1)}, f32[2,6144]{1,0:T(2,128)S(1)}, u32[]{:S(2)}, u32[]{:S(2)}) collective-permute-start(f32[2,6144]{1,0:T(2,128)S(1)} %pad_maximum_fusion), channel_id=1, source_target_pairs={{0,263},{1,256},{2,257},{3,258},{4,259},{5,260},{6,261},{7,262},{6... | collective-permute-start | bytes 147464 | tf_op jit(solution)/shard_map/ppermute | solution.py:297
  10.6 6.0 %copy-start.3 = (f32[1,16,4096]{2,1,0:T(8,128)S(1)}, f32[1,16,4096]{2,1,0:T(8,128)}, u32[]{:S(2)}) copy-start(f32[1,16,4096]{2,1,0:T(8,128)} %param.12) | copy-start | bytes 786436
  10.6 6.0 %copy-start.7 = (f32[1,16,4096]{2,1,0:T(8,128)S(1)}, f32[1,16,4096]{2,1,0:T(8,128)}, u32[]{:S(2)}) copy-start(f32[1,16,4096]{2,1,0:T(8,128)} %param.13) | copy-start | bytes 786436
  12.8 56.3 %collective-permute-start.5 = (bf16[128,2048]{1,0:T(8,128)(2,1)}, bf16[128,2048]{1,0:T(8,128)(2,1)S(1)}, u32[]{:S(2)}, u32[]{:S(2)}) collective-permute-start(bf16[128,2048]{1,0:T(8,128)(2,1)} %multiply_convert_fusion), channel_id=1, source_target_pairs={{0,7},{1,0},{2,1},{3,2},{4,3},{5,4},{6,5},{7,6},{8,15},{9,8},{10,9... | collective-permute-start | bytes 1572872 | tf_op jit(solution)/shard_map/ppermute | solution.py:281
  16.6 0.6 copy-start.8
  22.8 28.4 %copy-start.1 = (bf16[128,4096]{1,0:T(8,128)(2,1)S(1)}, bf16[128,4096]{1,0:T(8,128)(2,1)}, u32[]{:S(2)}) copy-start(bf16[128,4096]{1,0:T(8,128)(2,1)} %get-tuple-element.64.refs_0_) | copy-start | bytes 3145732 | tf_op jit(solution)/shard_map/cond
  36.8 12.3 %all-to-all-start.2 = ((f32[8,2,6144]{2,1,0:T(2,128)}), f32[8,2,6144]{2,1,0:T(2,128)S(1)}, u32[]{:S(2)}, u32[]{:S(2)}) async-start(f32[8,2,6144]{2,1,0:T(2,128)} %plane_sums.1), calls=%async_computation.2 | async-start | bytes 786432 | tf_op jit(solution)/shard_map/cond/branch_1_fun/all_to_all | solution.py:276
  49.1 2.1 %copy-start.2 = (f32[8,2,6144]{2,1,0:T(2,128)}, f32[8,2,6144]{2,1,0:T(2,128)S(1)}, u32[]{:S(2)}) copy-start(f32[8,2,6144]{2,1,0:T(2,128)S(1)} %all-to-all-done.2.refs_2_) | copy-start | bytes 1179652 | tf_op jit(solution)/shard_map/cond
  58.0 83.5 %collective-permute-start.6 = (bf16[128,2048]{1,0:T(8,128)(2,1)}, bf16[128,2048]{1,0:T(8,128)(2,1)S(1)}, u32[]{:S(2)}, u32[]{:S(2)}) collective-permute-start(bf16[128,2048]{1,0:T(8,128)(2,1)} %get-tuple-element.96), channel_id=1, source_target_pairs={{0,7},{1,0},{2,1},{3,2},{4,3},{5,4},{6,5},{7,6},{8,15},{9,8},{10,9... | collective-permute-start | bytes 1572872 | tf_op jit(solution)/shard_map/ppermute | solution.py:281
  87.2 22.5 %copy-start.9 = (f32[2,6144]{1,0:T(2,128)S(1)}, f32[2,6144]{1,0:T(2,128)}, u32[]{:S(2)}) copy-start(f32[2,6144]{1,0:T(2,128)} %get-tuple-element.71.param_ref) | copy-start | bytes 147460 | tf_op jit(solution)/shard_map/cond
  87.2 21.8 %all-to-all-start.4 = ((f32[8,2,2048]{2,1,0:T(2,128)}), f32[8,2,2048]{2,1,0:T(2,128)S(1)}, u32[]{:S(2)}, u32[]{:S(2)}) async-start(f32[8,2,2048]{2,1,0:T(2,128)} %early_states.1), calls=%async_computation.4 | async-start | bytes 262144 | tf_op jit(solution)/shard_map/cond/branch_1_fun/all_to_all | solution.py:276
  90.7 38.3 %collective-permute-start.3 = (bf16[4,4096]{1,0:T(4,128)(2,1)}, bf16[4,4096]{1,0:T(4,128)(2,1)}, u32[]{:S(2)}, u32[]{:S(2)}) collective-permute-start(bf16[4,4096]{1,0:T(4,128)(2,1)} %get-tuple-element.72), channel_id=1, source_target_pairs={{256,7},{257,0},{258,1},{259,2},{260,3},{261,4},{262,5},{263,6},{3... | collective-permute-start | bytes 98312 | tf_op jit(solution)/shard_map/cond/branch_1_fun/ppermute | solution.py:309
  95.0 33.9 %collective-permute-start.2 = (bf16[4,4096]{1,0:T(4,128)(2,1)}, bf16[4,4096]{1,0:T(4,128)(2,1)}, u32[]{:S(2)}, u32[]{:S(2)}) collective-permute-start(bf16[4,4096]{1,0:T(4,128)(2,1)} %get-tuple-element.72), channel_id=1, source_target_pairs={{192,7},{193,0},{194,1},{195,2},{196,3},{197,4},{198,5},{199,6},{2... | collective-permute-start | bytes 98312 | tf_op jit(solution)/shard_map/cond/branch_1_fun/ppermute | solution.py:309
  99.8 29.2 %collective-permute-start.1 = (bf16[4,4096]{1,0:T(4,128)(2,1)}, bf16[4,4096]{1,0:T(4,128)(2,1)}, u32[]{:S(2)}, u32[]{:S(2)}) collective-permute-start(bf16[4,4096]{1,0:T(4,128)(2,1)} %get-tuple-element.72), channel_id=1, source_target_pairs={{128,7},{129,0},{130,1},{131,2},{132,3},{133,4},{134,5},{135,6},{1... | collective-permute-start | bytes 98312 | tf_op jit(solution)/shard_map/cond/branch_1_fun/ppermute | solution.py:309
  102.5 26.5 %collective-permute-start = (bf16[4,4096]{1,0:T(4,128)(2,1)}, bf16[4,4096]{1,0:T(4,128)(2,1)}, u32[]{:S(2)}, u32[]{:S(2)}) collective-permute-start(bf16[4,4096]{1,0:T(4,128)(2,1)} %get-tuple-element.72), channel_id=1, source_target_pairs={{64,7},{65,0},{66,1},{67,2},{68,3},{69,4},{70,5},{71,6},{128,71},{... | collective-permute-start | bytes 98312 | tf_op jit(solution)/shard_map/cond/branch_1_fun/ppermute | solution.py:309
  109.0 0.7 copy-start.4
  111.3 10.8 %all-to-all-start.5 = ((f32[8,2,2048]{2,1,0:T(2,128)}), f32[8,2,2048]{2,1,0:T(2,128)S(1)}, u32[]{:S(2)}, u32[]{:S(2)}) async-start(f32[8,2,2048]{2,1,0:T(2,128)} %inner_entries.1), calls=%async_computation.5 | async-start | bytes 262144 | tf_op jit(solution)/shard_map/cond/branch_1_fun/all_to_all | solution.py:276
  122.1 0.7 copy-start.6
  141.5 0.8 copy-start.5

commit v4 on v3

--- a/solution.py
+++ b/solution.py
@@ -145,48 +145,40 @@
     )(states, rates, gains)
 
 
-def inner_kernel(state_ref, param_ref, entry_ref):
-    step = jnp.exp(-float(ROWS) * param_ref[:, :EARLY])
-    total = jnp.zeros_like(step)
-    for k in reversed(range(PLACES)):
-        entry_ref[k] = total
-        total = total * step + state_ref[k]
-
-
-def inner_entries(states, params):
-    return pl.pallas_call(
-        inner_kernel,
-        out_shape=jax.ShapeDtypeStruct(states.shape, F32),
-        name="inner_entries",
-    )(states, params)
-
-
-def outer_kernel(core_ref, rate_ref, *refs):
+def entry_kernel(core_ref, rate_ref, param_ref, state_ref, *refs):
     sum_refs, entry_ref = refs[:-1], refs[-1]
+    first = core_ref[0] == 0
     rates = rate_ref[...]
     stride = jnp.exp(-float(ROWS * PLACES) * rates)
     carry = sum_refs[-1][...].astype(F32)
     for sum_ref in sum_refs[-2::-1]:
         carry = carry * stride + sum_ref[...].astype(F32)
     beyond = jnp.exp(-float(ROWS * PLACES * HALF) * rates)
-    carry = jnp.where(core_ref[0] == 0, carry, carry * beyond)
+    carry = jnp.where(first, carry, carry * beyond)
     step = jnp.exp(-float(ROWS) * rates)
+    gains = param_ref[:, rates.shape[1] :]
+    early, late = carry[:, :EARLY], carry[:, EARLY:]
     for k in reversed(range(PLACES)):
-        entry_ref[k] = carry.astype(jnp.bfloat16)
-        carry = carry * step
-
-
-def outer_entries(core, rates, sums):
+        entry_ref[k, :, :EARLY] = early.astype(jnp.bfloat16)
+        entry_ref[k, :, EARLY:] = late.astype(jnp.bfloat16)
+        own = state_ref[k] * gains
+        own = jnp.concatenate([jnp.where(first, own, 0.0), jnp.where(first, 0.0, own)], axis=0)
+        early = early * step[:, :EARLY] + own
+        late = late * step[:, EARLY:]
+
+
+def block_entries(core, rates, params, states, sums):
     whole = pl.BlockSpec(memory_space=pltpu.VMEM)
     return pl.pallas_call(
-        outer_kernel,
-        in_specs=[pl.BlockSpec(memory_space=pltpu.SMEM)] + [whole] * (1 + len(sums)),
+        entry_kernel,
+        in_specs=[pl.BlockSpec(memory_space=pltpu.SMEM)] + [whole] * (3 + len(sums)),
         out_shape=jax.ShapeDtypeStruct((PLACES,) + rates.shape, jnp.bfloat16),
-        name="outer_entries",
-    )(core, rates, *sums)
-
-
-def sweep_kernel(sources, entry_ref, decay_ref, gain_ref, out_ref, source, result):
+        name="block_entries",
+    )(core, rates, params, states, *sums)
+
+
+def sweep_kernel(sources, *refs):
+    entry_refs, (decay_ref, gain_ref, out_ref, source, result) = refs[:-5], refs[-5:]
     sub = lax.broadcasted_iota(jnp.int32, (8, 128), 0)
 
     def one_group(group, _):
@@ -201,7 +193,8 @@
             part = source[pl.ds(i, 8, stride=16), :]
             held = [part if h is None else h * q + part for h, q in zip(held, keep)]
         for j in range(MODES):
-            value = jnp.where(sub == 7, mode_row(entry_ref, j, lanes), pltpu.roll(held[j], 7, 0))
+            enter = mode_row(entry_refs[0], j, lanes) if entry_refs else 0.0
+            value = jnp.where(sub == 7, enter, pltpu.roll(held[j], 7, 0))
             for shift in (1, 2, 4):
                 leap = jnp.where(sub < 8 - shift, jnp.exp(-16.0 * shift * rates[j]), 0.0)
                 value = value + leap * pltpu.roll(value, 8 - shift, 0)
@@ -329,16 +322,14 @@
     sums = [from_later(sums, k) for k in range(1, HALF + 1)]
     everywhere = exchange(jnp.broadcast_to(params[None], (PLACES,) + params.shape), "place")
     states = exchange(early_states([gated], everywhere, 0), "place")
-    entries = exchange(inner_entries(states, params), "place")
-    inputs = [(entries, 0), (everywhere, 0), (everywhere, channels)]
+    rows = sweep([gated], specs, counts, [(everywhere, 0), (everywhere, channels)], EARLY)
     chip = lax.axis_index("place") // 2 * 2
     rates = lax.dynamic_slice(everywhere, (chip, 0, 0), (2, SLOT, channels))
-    rates = rates.reshape(2 * SLOT, channels)
-    return sweep([gated], specs, counts, inputs, EARLY), everywhere, rates, sums
-
-
-def last_step(core, rates, sums):
-    return exchange(outer_entries(core, rates, sums), "place")
+    return rows, everywhere, rates.reshape(2 * SLOT, channels), states, sums
+
+
+def last_step(core, rates, params, states, sums):
+    return exchange(block_entries(core, rates, params, states, sums), "place")
 
 
 def shards(gate, grad, decay, amplitude):
@@ -354,10 +345,10 @@
     gate, grad, gated, params = lax.optimization_barrier((gate, grad, gated, params))
     local, sums = as_one_step(always, late_step, gate, grad, decay, gain, rates, gains)
     late_rows = passed_along(local, "section", -1)
-    early_rows, everywhere, rates, sums = as_one_step(
+    early_rows, everywhere, rates, states, sums = as_one_step(
         always, early_step, arrived, params, sums
     )
-    entries = as_one_step(always, last_step, core, rates, sums)
+    entries = as_one_step(always, last_step, core, rates, params, states, sums)
     return finish([early_rows, late_rows], entries, everywhere)[None]
 
 

time: 149 us -> 148 us (level)
  the two profiles are of different devices: /device:TPU:192 before, /device:TPU:448 now
where the time goes in v4:
time: 148 us; the launch traced here: 147 us
  starting transfers between devices  53.9 us (36%)
  Pallas kernels  30.6 us (21%)
  waiting for transfers between devices  30.1 us (20%)
  blocking collectives  23.1 us (16%)
  local copies, waits for them, and re-layouts  7.13 us (5%)
  other arithmetic  2.2 us (1%)
    all_to_all x2, blocking collectives, exchange(): return lax.all_to_all(values, axis, split_axis=0, concat_axis=0, tiled=True)  23.1 us
    ppermute x4, starting transfers between devices, from_later(): return lax.ppermute(sums, ('plane', 'place', 'section'), pairs)  23 us
    ppermute x4, waiting for transfers between devices, from_later(): return lax.ppermute(sums, ('plane', 'place', 'section'), pairs)  21.2 us
    ppermute x2, starting transfers between devices, passed_along(): lax.ppermute(shard, axis, [(i, (i + by) % count) for i in range(count)])  16.7 us
    pallas_call x2, Pallas kernels, sweep(): pl.pallas_call(in_parts(sweep_kernel, len(sources), counts), grid=(channe...  12.9 us
    all_to_all x3, starting transfers between devices, exchange(): return lax.all_to_all(values, axis, split_axis=0, concat_axis=0, tiled=True)  12.2 us
    all_to_all x3, waiting for transfers between devices, exchange(): return lax.all_to_all(values, axis, split_axis=0, concat_axis=0, tiled=True)  8.85 us
    pallas_call x1, Pallas kernels, all_states(): pl.pallas_call(in_parts(state_kernel, 2, [1]), grid=(channels // width,),...  5.57 us
  transfers between devices with their start and end apart: 10, of which 5 were waited for; matrix products, arithmetic and copies ran while one was open for 5% of the time, Pallas kernels for 17%

profile of v4, /device:TPU:448, one launch (start us, length us, event | category | flops | bytes accessed | tf_op | source)
XLA Modules:
  0.0 147.2 jit_solution(18355760655320119334)
XLA Ops:
  1.1 1.9 %collective-permute-start.4 = (f32[2,6144]{1,0:T(2,128)S(1)}, f32[2,6144]{1,0:T(2,128)S(1)}, u32[]{:S(2)}, u32[]{:S(2)}) collective-permute-start(f32[2,6144]{1,0:T(2,128)S(1)} %pad_maximum_fusion), channel_id=1, source_target_pairs={{0,263},{1,256},{2,257},{3,258},{4,259},{5,260},{6,261},{7,262},{6... | collective-permute-start | bytes 147464 | tf_op jit(solution)/shard_map/ppermute | solution.py:290
  3.1 2.2 %multiply_convert_fusion = bf16[128,2048]{1,0:T(8,128)(2,1)} fusion(bf16[128,4096]{1,0:T(8,128)(2,1)} %bitcast.10, bf16[128,4096]{1,0:T(8,128)(2,1)} %bitcast.12), kind=kLoop, calls=%fused_computation.2 | loop fusion | flops 1048576 | bytes 1572864 | tf_op jit(solution)/shard_map/convert_element_type | solution.py:343
  5.3 13.0 %collective-permute-start.5 = (bf16[128,2048]{1,0:T(8,128)(2,1)}, bf16[128,2048]{1,0:T(8,128)(2,1)S(1)}, u32[]{:S(2)}, u32[]{:S(2)}) collective-permute-start(bf16[128,2048]{1,0:T(8,128)(2,1)} %multiply_convert_fusion), channel_id=1, source_target_pairs={{0,7},{1,0},{2,1},{3,2},{4,3},{5,4},{6,5},{7,6},{8,15},{9,8},{10,9... | collective-permute-start | bytes 1572872 | tf_op jit(solution)/shard_map/ppermute | solution.py:274
  18.9 40.7 %conditional.3 = (bf16[128,2048]{1,0:T(8,128)(2,1)}, bf16[4,4096]{1,0:T(4,128)(2,1)}) conditional(s32[]{:T(128)} %convert_element_type.20, () %tuple.33, (f32[1,16,4096]{2,1,0:T(8,128)S(1)}, bf16[128,4096]{1,0:T(8,128)(2,1)}, bf16[128,4096]{1,0:T(8,128)(2,1)S(1)}, f32[2,4096]{1,0:T(2,128)S(1)}, f32[2,4096]{1,0:T(2,128)S(1)}, ...), branch_computations={%region_0.1_spmd, %region_1.2_spmd} | conditional | flops 22 | bytes 7602512 | solution.py:280
  18.9 5.6 %all_states.1 = f32[8,2,4096]{2,1,0:T(2,128)} custom-call(bf16[128,4096]{1,0:T(8,128)(2,1)} %get-tuple-element.68.refs_0_, bf16[128,4096]{1,0:T(8,128)(2,1)S(1)} %get-tuple-element.69.refs_1_, f32[16,4096]{1,0:T(8,128)S(1)} %bitcast.14), custom_call_target="tpu_custom_call" | custom-call | tf_op jit(solution)/shard_map/cond/branch_1_fun/all_states/pallas_call | solution.py:105
  24.5 12.2 %all_to_all.20.state_ref = f32[8,2,4096]{2,1,0:T(2,128)} all-to-all(f32[8,2,4096]{2,1,0:T(2,128)} %all_states.1), channel_id=1, replica_groups=mesh['plane'=8,'place'=8,'section'=8] {'place'}, dimensions={0} | all-to-all | bytes 524288 | tf_op jit(solution)/shard_map/cond/branch_1_fun/all_to_all | solution.py:269
  38.5 3.5 %all-to-all-start.2 = ((f32[8,2,6144]{2,1,0:T(2,128)}), f32[8,2,6144]{2,1,0:T(2,128)S(1)}, u32[]{:S(2)}, u32[]{:S(2)}) async-start(f32[8,2,6144]{2,1,0:T(2,128)} %plane_sums.1), calls=%async_computation.2 | async-start | bytes 786432 | tf_op jit(solution)/shard_map/cond/branch_1_fun/all_to_all | solution.py:269
  42.0 8.8 %all-to-all-done.2.refs_2_ = f32[8,2,6144]{2,1,0:T(2,128)S(1)} async-done(((f32[8,2,6144]{2,1,0:T(2,128)}), f32[8,2,6144]{2,1,0:T(2,128)S(1)}, u32[]{:S(2)}, u32[]{:S(2)}) %all-to-all-start.2) | async-done | bytes 393248 | tf_op jit(solution)/shard_map/cond/branch_1_fun/all_to_all | solution.py:269
  52.9 6.8 %sweep.2 = bf16[128,2048]{1,0:T(8,128)(2,1)} custom-call(bf16[128,4096]{1,0:T(8,128)(2,1)S(1)} %copy-done.1, bf16[128,4096]{1,0:T(8,128)(2,1)S(1)} %get-tuple-element.69.refs_1_, f32[8,2,6144]{2,1,0:T(2,128)} %copy-done.2, f32[16,4096]{1,0:T(8,128)S(1)} %bitcast.15, f32[16,4096]{1,0:T(8,128)S(1)} %bitcast.16), custom_call_target="tpu_custom_call" | custom-call | tf_op jit(solution)/shard_map/cond/branch_1_fun/sweep/pallas_call | solution.py:219
  59.6 3.7 %collective-permute-start.6 = (bf16[128,2048]{1,0:T(8,128)(2,1)}, bf16[128,2048]{1,0:T(8,128)(2,1)S(1)}, u32[]{:S(2)}, u32[]{:S(2)}) collective-permute-start(bf16[128,2048]{1,0:T(8,128)(2,1)} %get-tuple-element.103), channel_id=1, source_target_pairs={{0,7},{1,0},{2,1},{3,2},{4,3},{5,4},{6,5},{7,6},{8,15},{9,8},{10,9... | collective-permute-start | bytes 1572872 | tf_op jit(solution)/shard_map/ppermute | solution.py:274
  63.4 65.1 %conditional.4 = (bf16[128,2048]{1,0:T(8,128)(2,1)S(1)}, f32[8,2,6144]{2,1,0:T(2,128)}, f32[4,4096]{1,0:T(4,128)S(1)}, f32[8,2,2048]{2,1,0:T(2,128)}, bf16[4,409...) conditional(s32[]{:T(128)} %convert_element_type.20, () %tuple.31, ...), branch_computations={%region_2.3_spmd, %region_3.4_spmd} | conditional | flops 22 | bytes 2802184 | solution.py:280
  65.0 4.1 %all-to-all-start.3 = ((f32[8,2,6144]{2,1,0:T(2,128)}), f32[8,2,6144]{2,1,0:T(2,128)}, u32[]{:S(2)}, u32[]{:S(2)}) async-start(f32[8,2,6144]{2,1,0:T(2,128)} %broadcast_in_dim.0), calls=%async_computation.3 | async-start | bytes 786432 | tf_op jit(solution)/shard_map/cond/branch_1_fun/all_to_all | solution.py:269
  69.2 11.1 %collective-permute-start.3 = (bf16[4,4096]{1,0:T(4,128)(2,1)}, bf16[4,4096]{1,0:T(4,128)(2,1)}, u32[]{:S(2)}, u32[]{:S(2)}) collective-permute-start(bf16[4,4096]{1,0:T(4,128)(2,1)} %get-tuple-element.76), channel_id=1, source_target_pairs={{256,7},{257,0},{258,1},{259,2},{260,3},{261,4},{262,5},{263,6},{3... | collective-permute-start | bytes 98312 | tf_op jit(solution)/shard_map/cond/branch_1_fun/ppermute | solution.py:302
  80.3 3.2 %collective-permute-start.2 = (bf16[4,4096]{1,0:T(4,128)(2,1)}, bf16[4,4096]{1,0:T(4,128)(2,1)}, u32[]{:S(2)}, u32[]{:S(2)}) collective-permute-start(bf16[4,4096]{1,0:T(4,128)(2,1)} %get-tuple-element.76), channel_id=1, source_target_pairs={{192,7},{193,0},{194,1},{195,2},{196,3},{197,4},{198,5},{199,6},{2... | collective-permute-start | bytes 98312 | tf_op jit(solution)/shard_map/cond/branch_1_fun/ppermute | solution.py:302
  83.5 1.9 %collective-permute-start.1 = (bf16[4,4096]{1,0:T(4,128)(2,1)}, bf16[4,4096]{1,0:T(4,128)(2,1)}, u32[]{:S(2)}, u32[]{:S(2)}) collective-permute-start(bf16[4,4096]{1,0:T(4,128)(2,1)} %get-tuple-element.76), channel_id=1, source_target_pairs={{128,7},{129,0},{130,1},{131,2},{132,3},{133,4},{134,5},{135,6},{1... | collective-permute-start | bytes 98312 | tf_op jit(solution)/shard_map/cond/branch_1_fun/ppermute | solution.py:302
  85.4 6.8 %collective-permute-start = (bf16[4,4096]{1,0:T(4,128)(2,1)}, bf16[4,4096]{1,0:T(4,128)(2,1)}, u32[]{:S(2)}, u32[]{:S(2)}) collective-permute-start(bf16[4,4096]{1,0:T(4,128)(2,1)} %get-tuple-element.76), channel_id=1, source_target_pairs={{64,7},{65,0},{66,1},{67,2},{68,3},{69,4},{70,5},{71,6},{128,71},{... | collective-permute-start | bytes 98312 | tf_op jit(solution)/shard_map/cond/branch_1_fun/ppermute | solution.py:302
  92.2 3.3 %early_states.1 = f32[8,2,2048]{2,1,0:T(2,128)} custom-call(bf16[128,2048]{1,0:T(8,128)(2,1)S(1)} %get-tuple-element.74.refs_0_, f32[8,2,6144]{2,1,0:T(2,128)} %all-to-all-done.3.refs_1_.refs_2_), custom_call_target="tpu_custom_call" | custom-call | tf_op jit(solution)/shard_map/cond/branch_1_fun/early_states/pallas_call | solution.py:117
  95.5 4.7 %all-to-all-start.4 = ((f32[8,2,2048]{2,1,0:T(2,128)}), f32[8,2,2048]{2,1,0:T(2,128)}, u32[]{:S(2)}, u32[]{:S(2)}) async-start(f32[8,2,2048]{2,1,0:T(2,128)} %early_states.1), calls=%async_computation.4 | async-start | bytes 262144 | tf_op jit(solution)/shard_map/cond/branch_1_fun/all_to_all | solution.py:269
  101.1 6.2 %sweep.3 = bf16[128,2048]{1,0:T(8,128)(2,1)S(1)} custom-call(bf16[128,2048]{1,0:T(8,128)(2,1)S(1)} %get-tuple-element.74.refs_0_, f32[8,2,6144]{2,1,0:T(2,128)} %all-to-all-done.3.refs_1_.refs_2_, f32[8,2,6144]{2,1,0:T(2,128)} %all-to-all-done.3.refs_1_.refs_2_), custom_call_target="tpu_custom_call" | custom-call | tf_op jit(solution)/shard_map/cond/branch_1_fun/sweep/pallas_call | solution.py:219
  107.3 8.7 %collective-permute-done.3 = bf16[4,4096]{1,0:T(4,128)(2,1)} collective-permute-done((bf16[4,4096]{1,0:T(4,128)(2,1)}, bf16[4,4096]{1,0:T(4,128)(2,1)}, u32[]{:S(2)}, u32[]{:S(2)}) %collective-permute-start.3) | collective-permute-done | bytes 32800 | tf_op jit(solution)/shard_map/cond/branch_1_fun/ppermute | solution.py:302
  116.9 11.6 %collective-permute-done = bf16[4,4096]{1,0:T(4,128)(2,1)} collective-permute-done((bf16[4,4096]{1,0:T(4,128)(2,1)}, bf16[4,4096]{1,0:T(4,128)(2,1)}, u32[]{:S(2)}, u32[]{:S(2)}) %collective-permute-start) | collective-permute-done | bytes 32800 | tf_op jit(solution)/shard_map/cond/branch_1_fun/ppermute | solution.py:302
  128.5 12.7 %conditional.5 = (bf16[8,4,4096]{2,1,0:T(4,128)(2,1)S(1)}) conditional(s32[]{:T(128)} %convert_element_type.20, () %tuple.36, (s32[]{:T(128)}, f32[4,4096]{1,0:T(4,128)S(1)}, f32[2,6144]{1,0:T(2,128)}, f32[8,2,2048]{2,1,0:T(2,128)}, bf16[4,4096]{1,0:T(4,128)(2,1)}, /*index=5*/bf16[4,4096]{1,0:T(4,128)(2,1)}, bf16[4,4096]{1,0:T(4,128)(2,1)}, ...), branch_computations={%region_4.5_spmd, %region_5.6_spmd} | conditional | flops 11 | bytes 524405 | solution.py:280
  130.3 10.8 %all_to_all.21 = bf16[8,4,4096]{2,1,0:T(4,128)(2,1)S(1)} all-to-all(bf16[8,4,4096]{2,1,0:T(4,128)(2,1)} %block_entries.1), channel_id=1, replica_groups=mesh['plane'=8,'place'=8,'section'=8] {'place'}, dimensions={0} | all-to-all | bytes 524288 | tf_op jit(solution)/shard_map/cond/branch_1_fun/all_to_all | solution.py:269
  142.0 5.2 %finish.1 = bf16[128,4096]{1,0:T(8,128)(2,1)} custom-call(bf16[128,2048]{1,0:T(8,128)(2,1)S(1)} %get-tuple-element.102.refs_0_, bf16[128,2048]{1,0:T(8,128)(2,1)} %copy-done.4, bf16[8,4,4096]{2,1,0:T(4,128)(2,1)S(1)} %get-tuple-element.133.refs_2_, f32[8,2,6144]{2,1,0:T(2,128)} %get-tuple-element.110.refs_3_), custom_call_target="tpu_custom_call" | custom-call | tf_op jit(solution)/shard_map/finish/pallas_call | solution.py:258
  (31 shorter events, 11.7 us)
Async XLA Ops:
  0.0 18.3 %copy-start = (bf16[1,128,4096]{2,1,0:T(8,128)(2,1)S(1)}, bf16[1,128,4096]{2,1,0:T(8,128)(2,1)}, u32[]{:S(2)}) copy-start(bf16[1,128,4096]{2,1,0:T(8,128)(2,1)} %param.11) | copy-start | bytes 3145732
  1.1 17.1 %collective-permute-start.4 = (f32[2,6144]{1,0:T(2,128)S(1)}, f32[2,6144]{1,0:T(2,128)S(1)}, u32[]{:S(2)}, u32[]{:S(2)}) collective-permute-start(f32[2,6144]{1,0:T(2,128)S(1)} %pad_maximum_fusion), channel_id=1, source_target_pairs={{0,263},{1,256},{2,257},{3,258},{4,259},{5,260},{6,261},{7,262},{6... | collective-permute-start | bytes 147464 | tf_op jit(solution)/shard_map/ppermute | solution.py:290
  3.1 15.2 %copy-start.3 = (f32[1,16,4096]{2,1,0:T(8,128)S(1)}, f32[1,16,4096]{2,1,0:T(8,128)}, u32[]{:S(2)}) copy-start(f32[1,16,4096]{2,1,0:T(8,128)} %param.12) | copy-start | bytes 786436
  3.1 15.2 %copy-start.5 = (f32[1,16,4096]{2,1,0:T(8,128)S(1)}, f32[1,16,4096]{2,1,0:T(8,128)}, u32[]{:S(2)}) copy-start(f32[1,16,4096]{2,1,0:T(8,128)} %param.13) | copy-start | bytes 786436
  5.3 58.1 %collective-permute-start.5 = (bf16[128,2048]{1,0:T(8,128)(2,1)}, bf16[128,2048]{1,0:T(8,128)(2,1)S(1)}, u32[]{:S(2)}, u32[]{:S(2)}) collective-permute-start(bf16[128,2048]{1,0:T(8,128)(2,1)} %multiply_convert_fusion), channel_id=1, source_target_pairs={{0,7},{1,0},{2,1},{3,2},{4,3},{5,4},{6,5},{7,6},{8,15},{9,8},{10,9... | collective-permute-start | bytes 1572872 | tf_op jit(solution)/shard_map/ppermute | solution.py:274
  18.3 0.6 copy-start.6
  24.5 28.4 %copy-start.1 = (bf16[128,4096]{1,0:T(8,128)(2,1)S(1)}, bf16[128,4096]{1,0:T(8,128)(2,1)}, u32[]{:S(2)}) copy-start(bf16[128,4096]{1,0:T(8,128)(2,1)} %get-tuple-element.68.refs_0_) | copy-start | bytes 3145732 | tf_op jit(solution)/shard_map/cond
  38.5 12.3 %all-to-all-start.2 = ((f32[8,2,6144]{2,1,0:T(2,128)}), f32[8,2,6144]{2,1,0:T(2,128)S(1)}, u32[]{:S(2)}, u32[]{:S(2)}) async-start(f32[8,2,6144]{2,1,0:T(2,128)} %plane_sums.1), calls=%async_computation.2 | async-start | bytes 786432 | tf_op jit(solution)/shard_map/cond/branch_1_fun/all_to_all | solution.py:269
  50.8 2.1 %copy-start.2 = (f32[8,2,6144]{2,1,0:T(2,128)}, f32[8,2,6144]{2,1,0:T(2,128)S(1)}, u32[]{:S(2)}) copy-start(f32[8,2,6144]{2,1,0:T(2,128)S(1)} %all-to-all-done.2.refs_2_) | copy-start | bytes 1179652 | tf_op jit(solution)/shard_map/cond
  59.6 81.5 %collective-permute-start.6 = (bf16[128,2048]{1,0:T(8,128)(2,1)}, bf16[128,2048]{1,0:T(8,128)(2,1)S(1)}, u32[]{:S(2)}, u32[]{:S(2)}) collective-permute-start(bf16[128,2048]{1,0:T(8,128)(2,1)} %get-tuple-element.103), channel_id=1, source_target_pairs={{0,7},{1,0},{2,1},{3,2},{4,3},{5,4},{6,5},{7,6},{8,15},{9,8},{10,9... | collective-permute-start | bytes 1572872 | tf_op jit(solution)/shard_map/ppermute | solution.py:274
  65.0 27.2 %all-to-all-start.3 = ((f32[8,2,6144]{2,1,0:T(2,128)}), f32[8,2,6144]{2,1,0:T(2,128)}, u32[]{:S(2)}, u32[]{:S(2)}) async-start(f32[8,2,6144]{2,1,0:T(2,128)} %broadcast_in_dim.0), calls=%async_computation.3 | async-start | bytes 786432 | tf_op jit(solution)/shard_map/cond/branch_1_fun/all_to_all | solution.py:269
  69.2 46.8 %collective-permute-start.3 = (bf16[4,4096]{1,0:T(4,128)(2,1)}, bf16[4,4096]{1,0:T(4,128)(2,1)}, u32[]{:S(2)}, u32[]{:S(2)}) collective-permute-start(bf16[4,4096]{1,0:T(4,128)(2,1)} %get-tuple-element.76), channel_id=1, source_target_pairs={{256,7},{257,0},{258,1},{259,2},{260,3},{261,4},{262,5},{263,6},{3... | collective-permute-start | bytes 98312 | tf_op jit(solution)/shard_map/cond/branch_1_fun/ppermute | solution.py:302
  80.3 36.3 %collective-permute-start.2 = (bf16[4,4096]{1,0:T(4,128)(2,1)}, bf16[4,4096]{1,0:T(4,128)(2,1)}, u32[]{:S(2)}, u32[]{:S(2)}) collective-permute-start(bf16[4,4096]{1,0:T(4,128)(2,1)} %get-tuple-element.76), channel_id=1, source_target_pairs={{192,7},{193,0},{194,1},{195,2},{196,3},{197,4},{198,5},{199,6},{2... | collective-permute-start | bytes 98312 | tf_op jit(solution)/shard_map/cond/branch_1_fun/ppermute | solution.py:302
  83.5 33.4 %collective-permute-start.1 = (bf16[4,4096]{1,0:T(4,128)(2,1)}, bf16[4,4096]{1,0:T(4,128)(2,1)}, u32[]{:S(2)}, u32[]{:S(2)}) collective-permute-start(bf16[4,4096]{1,0:T(4,128)(2,1)} %get-tuple-element.76), channel_id=1, source_target_pairs={{128,7},{129,0},{130,1},{131,2},{132,3},{133,4},{134,5},{135,6},{1... | collective-permute-start | bytes 98312 | tf_op jit(solution)/shard_map/cond/branch_1_fun/ppermute | solution.py:302
  85.4 43.1 %collective-permute-start = (bf16[4,4096]{1,0:T(4,128)(2,1)}, bf16[4,4096]{1,0:T(4,128)(2,1)}, u32[]{:S(2)}, u32[]{:S(2)}) collective-permute-start(bf16[4,4096]{1,0:T(4,128)(2,1)} %get-tuple-element.76), channel_id=1, source_target_pairs={{64,7},{65,0},{66,1},{67,2},{68,3},{69,4},{70,5},{71,6},{128,71},{... | collective-permute-start | bytes 98312 | tf_op jit(solution)/shard_map/cond/branch_1_fun/ppermute | solution.py:302
  95.5 33.0 %all-to-all-start.4 = ((f32[8,2,2048]{2,1,0:T(2,128)}), f32[8,2,2048]{2,1,0:T(2,128)}, u32[]{:S(2)}, u32[]{:S(2)}) async-start(f32[8,2,2048]{2,1,0:T(2,128)} %early_states.1), calls=%async_computation.4 | async-start | bytes 262144 | tf_op jit(solution)/shard_map/cond/branch_1_fun/all_to_all | solution.py:269
  141.2 0.8 copy-start.4

commit v5 on v4

--- a/solution.py
+++ b/solution.py
@@ -307,23 +307,22 @@
     late = channels - EARLY
     states = exchange(all_states(gate, grad, decay), "place")
     spread = exchange(plane_sums(states, rates, gains), "place")
-    chip = lax.axis_index("place") // 2 * 2
-    sums = lax.dynamic_slice(spread, (chip, 0, late), (2, SLOT, channels))
-    sums = sums.reshape(2 * SLOT, channels).astype(jnp.bfloat16)
     sources = [gate, grad]
     specs = [columns(s.shape, EARLY) for s in sources]
     inputs = [(spread, 0), (decay, EARLY), (gain, EARLY)]
-    return sweep(sources, specs, [1], inputs, late), sums
-
-
-def early_step(gated, params, sums):
+    return sweep(sources, specs, [1], inputs, late), spread
+
+
+def early_step(gated, params, spread):
     specs, counts = part_columns([gated])
     channels = params.shape[1] - EARLY
+    chip = lax.axis_index("place") // 2 * 2
+    sums = lax.dynamic_slice(spread, (chip, 0, channels - EARLY), (2, SLOT, channels))
+    sums = sums.reshape(2 * SLOT, channels).astype(jnp.bfloat16)
     sums = [from_later(sums, k) for k in range(1, HALF + 1)]
     everywhere = exchange(jnp.broadcast_to(params[None], (PLACES,) + params.shape), "place")
     states = exchange(early_states([gated], everywhere, 0), "place")
     rows = sweep([gated], specs, counts, [(everywhere, 0), (everywhere, channels)], EARLY)
-    chip = lax.axis_index("place") // 2 * 2
     rates = lax.dynamic_slice(everywhere, (chip, 0, 0), (2, SLOT, channels))
     return rows, everywhere, rates.reshape(2 * SLOT, channels), states, sums
 
@@ -343,10 +342,10 @@
     gated = (gate[:, :EARLY].astype(F32) * grad[:, :EARLY].astype(F32)).astype(jnp.bfloat16)
     arrived = passed_along(gated, "section", -1)
     gate, grad, gated, params = lax.optimization_barrier((gate, grad, gated, params))
-    local, sums = as_one_step(always, late_step, gate, grad, decay, gain, rates, gains)
+    local, spread = as_one_step(always, late_step, gate, grad, decay, gain, rates, gains)
     late_rows = passed_along(local, "section", -1)
     early_rows, everywhere, rates, states, sums = as_one_step(
-        always, early_step, arrived, params, sums
+        always, early_step, arrived, params, spread
     )
     entries = as_one_step(always, last_step, core, rates, params, states, sums)
     return finish([early_rows, late_rows], entries, everywhere)[None]

time: 148 us -> 148 us (level)
  the two profiles are of different devices: /device:TPU:448 before, /device:TPU:64 now
where the time goes in v5:
time: 148 us; the launch traced here: 146 us
  starting transfers between devices  43.9 us (30%)
  blocking collectives  39.5 us (27%)
  Pallas kernels  30.6 us (21%)
  waiting for transfers between devices  25.4 us (17%)
  local copies, waits for them, and re-layouts  4.55 us (3%)
  other arithmetic  2.2 us (1%)
    all_to_all x3, blocking collectives, exchange(): return lax.all_to_all(values, axis, split_axis=0, concat_axis=0, tiled=True)  39.5 us
    ppermute x4, waiting for transfers between devices, from_later(): return lax.ppermute(sums, ('plane', 'place', 'section'), pairs)  19.8 us
    ppermute x2, starting transfers between devices, passed_along(): lax.ppermute(shard, axis, [(i, (i + by) % count) for i in range(count)])  14.8 us
    ppermute x1, starting transfers between devices, half_ring(): return lax.ppermute(message, ('plane', 'section'), pairs)  13.1 us
    pallas_call x2, Pallas kernels, sweep(): pl.pallas_call(in_parts(sweep_kernel, len(sources), counts), grid=(channe...  12.9 us
    all_to_all x2, starting transfers between devices, exchange(): return lax.all_to_all(values, axis, split_axis=0, concat_axis=0, tiled=True)  9.53 us
    ppermute x4, starting transfers between devices, from_later(): return lax.ppermute(sums, ('plane', 'place', 'section'), pairs)  6.43 us
    pallas_call x1, Pallas kernels, all_states(): pl.pallas_call(in_parts(state_kernel, 2, [1]), grid=(channels // width,),...  5.59 us
  transfers between devices with their start and end apart: 9, of which 4 were waited for; matrix products, arithmetic and copies ran while one was open for 3% of the time, Pallas kernels for 17%

profile of v5, /device:TPU:64, one launch (start us, length us, event | category | flops | bytes accessed | tf_op | source)
XLA Modules:
  0.0 146.4 jit_solution(18280938317601055969)
XLA Ops:
  1.1 13.1 %collective-permute-start.4 = (f32[2,6144]{1,0:T(2,128)S(1)}, f32[2,6144]{1,0:T(2,128)S(1)}, u32[]{:S(2)}, u32[]{:S(2)}) collective-permute-start(f32[2,6144]{1,0:T(2,128)S(1)} %pad_maximum_fusion), channel_id=1, source_target_pairs={{0,263},{1,256},{2,257},{3,258},{4,259},{5,260},{6,261},{7,262},{6... | collective-permute-start | bytes 147464 | tf_op jit(solution)/shard_map/ppermute | solution.py:290
  14.3 2.2 %multiply_convert_fusion = bf16[128,2048]{1,0:T(8,128)(2,1)} fusion(bf16[128,4096]{1,0:T(8,128)(2,1)} %bitcast.10, bf16[128,4096]{1,0:T(8,128)(2,1)} %bitcast.12), kind=kLoop, calls=%fused_computation.2 | loop fusion | flops 1048576 | bytes 1572864 | tf_op jit(solution)/shard_map/convert_element_type | solution.py:342
  16.5 5.4 %collective-permute-start.5 = (bf16[128,2048]{1,0:T(8,128)(2,1)}, bf16[128,2048]{1,0:T(8,128)(2,1)S(1)}, u32[]{:S(2)}, u32[]{:S(2)}) collective-permute-start(bf16[128,2048]{1,0:T(8,128)(2,1)} %multiply_convert_fusion), channel_id=1, source_target_pairs={{0,7},{1,0},{2,1},{3,2},{4,3},{5,4},{6,5},{7,6},{8,15},{9,8},{10,9... | collective-permute-start | bytes 1572872 | tf_op jit(solution)/shard_map/ppermute | solution.py:274
  21.9 39.4 %conditional.3 = (bf16[128,2048]{1,0:T(8,128)(2,1)}, f32[8,2,6144]{2,1,0:T(2,128)}) conditional(s32[]{:T(128)} %convert_element_type.20, () %tuple.33, (f32[1,16,4096]{2,1,0:T(8,128)S(1)}, bf16[128,4096]{1,0:T(8,128)(2,1)}, bf16[128,4096]{1,0:T(8,128)(2,1)S(1)}, f32[2,4096]{1,0:T(2,128)S(1)}, f32[2,4096]{1,0:T(2,128)S(1)}, ...), branch_computations={%region_0.1_spmd, %region_1.2_spmd} | conditional | bytes 5505068 | solution.py:280
  22.0 5.6 %all_states.1 = f32[8,2,4096]{2,1,0:T(2,128)} custom-call(bf16[128,4096]{1,0:T(8,128)(2,1)} %get-tuple-element.68.refs_0_, bf16[128,4096]{1,0:T(8,128)(2,1)S(1)} %get-tuple-element.69.refs_1_, f32[16,4096]{1,0:T(8,128)S(1)} %bitcast.14), custom_call_target="tpu_custom_call" | custom-call | tf_op jit(solution)/shard_map/cond/branch_1_fun/all_states/pallas_call | solution.py:105
  27.5 12.2 %all_to_all.20.state_ref = f32[8,2,4096]{2,1,0:T(2,128)} all-to-all(f32[8,2,4096]{2,1,0:T(2,128)} %all_states.1), channel_id=1, replica_groups=mesh['plane'=8,'place'=8,'section'=8] {'place'}, dimensions={0} | all-to-all | bytes 524288 | tf_op jit(solution)/shard_map/cond/branch_1_fun/all_to_all | solution.py:269
  39.8 1.7 %plane_sums.1 = f32[8,2,6144]{2,1,0:T(2,128)} custom-call(f32[8,2,4096]{2,1,0:T(2,128)} %all_to_all.20.state_ref, f32[2,4096]{1,0:T(2,128)S(1)} %get-tuple-element.71.rate_ref, f32[2,4096]{1,0:T(2,128)S(1)} %get-tuple-element.72.gain_ref), custom_call_target="tpu_custom_call" | custom-call | tf_op jit(solution)/shard_map/cond/branch_1_fun/plane_sums/pallas_call | solution.py:141
  41.5 13.0 %all_to_all.21.refs_2_ = f32[8,2,6144]{2,1,0:T(2,128)} all-to-all(f32[8,2,6144]{2,1,0:T(2,128)} %plane_sums.1), channel_id=1, replica_groups=mesh['plane'=8,'place'=8,'section'=8] {'place'}, dimensions={0} | all-to-all | bytes 786432 | tf_op jit(solution)/shard_map/cond/branch_1_fun/all_to_all | solution.py:269
  54.6 6.8 %sweep.2 = bf16[128,2048]{1,0:T(8,128)(2,1)} custom-call(bf16[128,4096]{1,0:T(8,128)(2,1)S(1)} %copy-done.1, bf16[128,4096]{1,0:T(8,128)(2,1)S(1)} %get-tuple-element.69.refs_1_, f32[8,2,6144]{2,1,0:T(2,128)} %all_to_all.21.refs_2_, f32[16,4096]{1,0:T(8,128)S(1)} %bitcast.15, f32[16,4096]{1,0:T(8,128)S(1)} %bitcast.16), custom_call_target="tpu_custom_call" | custom-call | tf_op jit(solution)/shard_map/cond/branch_1_fun/sweep/pallas_call | solution.py:219
  61.3 9.4 %collective-permute-start.6 = (bf16[128,2048]{1,0:T(8,128)(2,1)}, bf16[128,2048]{1,0:T(8,128)(2,1)S(1)}, u32[]{:S(2)}, u32[]{:S(2)}) collective-permute-start(bf16[128,2048]{1,0:T(8,128)(2,1)} %get-tuple-element.103), channel_id=1, source_target_pairs={{0,7},{1,0},{2,1},{3,2},{4,3},{5,4},{6,5},{7,6},{8,15},{9,8},{10,9... | collective-permute-start | bytes 1572872 | tf_op jit(solution)/shard_map/ppermute | solution.py:274
  70.7 3.9 %collective-permute-done.5 = bf16[128,2048]{1,0:T(8,128)(2,1)S(1)} collective-permute-done((bf16[128,2048]{1,0:T(8,128)(2,1)}, bf16[128,2048]{1,0:T(8,128)(2,1)S(1)}, u32[]{:S(2)}, u32[]{:S(2)}) %collective-permute-start.5) | collective-permute-done | bytes 524320 | tf_op jit(solution)/shard_map/ppermute | solution.py:274
  74.6 49.6 %conditional.4 = (bf16[128,2048]{1,0:T(8,128)(2,1)S(1)}, f32[8,2,6144]{2,1,0:T(2,128)}, f32[4,4096]{1,0:T(4,128)S(1)}, f32[8,2,2048]{2,1,0:T(2,128)}, bf16[4,409...) conditional(s32[]{:T(128)} %convert_element_type.20, () %tuple.31, ...), branch_computations={%region_2.3_spmd, %region_3.4_spmd} | conditional | flops 22 | bytes 2933260 | solution.py:280
  75.4 5.5 %all-to-all-start.3 = ((f32[8,2,6144]{2,1,0:T(2,128)}), f32[8,2,6144]{2,1,0:T(2,128)}, u32[]{:S(2)}, u32[]{:S(2)}) async-start(f32[8,2,6144]{2,1,0:T(2,128)} %broadcast_in_dim.0), calls=%async_computation.3 | async-start | bytes 786432 | tf_op jit(solution)/shard_map/cond/branch_1_fun/all_to_all | solution.py:269
  84.5 1.9 %collective-permute-start.1 = (bf16[4,4096]{1,0:T(4,128)(2,1)S(1)}, bf16[4,4096]{1,0:T(4,128)(2,1)}, u32[]{:S(2)}, u32[]{:S(2)}) collective-permute-start(bf16[4,4096]{1,0:T(4,128)(2,1)S(1)} %convert_element_type.15), channel_id=1, source_target_pairs={{128,7},{129,0},{130,1},{131,2},{132,3},{133,4},{134,5},{135,6},{1... | collective-permute-start | bytes 98312 | tf_op jit(solution)/shard_map/cond/branch_1_fun/ppermute | solution.py:302
  86.4 1.9 %collective-permute-start = (bf16[4,4096]{1,0:T(4,128)(2,1)S(1)}, bf16[4,4096]{1,0:T(4,128)(2,1)}, u32[]{:S(2)}, u32[]{:S(2)}) collective-permute-start(bf16[4,4096]{1,0:T(4,128)(2,1)S(1)} %convert_element_type.15), channel_id=1, source_target_pairs={{64,7},{65,0},{66,1},{67,2},{68,3},{69,4},{70,5},{71,6},{128,71},{... | collective-permute-start | bytes 98312 | tf_op jit(solution)/shard_map/cond/branch_1_fun/ppermute | solution.py:302
  90.0 3.2 %early_states.1 = f32[8,2,2048]{2,1,0:T(2,128)} custom-call(bf16[128,2048]{1,0:T(8,128)(2,1)S(1)} %get-tuple-element.74.refs_0_, f32[8,2,6144]{2,1,0:T(2,128)} %all-to-all-done.3.refs_1_.refs_2_), custom_call_target="tpu_custom_call" | custom-call | tf_op jit(solution)/shard_map/cond/branch_1_fun/early_states/pallas_call | solution.py:117
  93.3 4.0 %all-to-all-start.4 = ((f32[8,2,2048]{2,1,0:T(2,128)}), f32[8,2,2048]{2,1,0:T(2,128)}, u32[]{:S(2)}, u32[]{:S(2)}) async-start(f32[8,2,2048]{2,1,0:T(2,128)} %early_states.1), calls=%async_computation.4 | async-start | bytes 262144 | tf_op jit(solution)/shard_map/cond/branch_1_fun/all_to_all | solution.py:269
  98.2 6.2 %sweep.3 = bf16[128,2048]{1,0:T(8,128)(2,1)S(1)} custom-call(bf16[128,2048]{1,0:T(8,128)(2,1)S(1)} %get-tuple-element.74.refs_0_, f32[8,2,6144]{2,1,0:T(2,128)} %all-to-all-done.3.refs_1_.refs_2_, f32[8,2,6144]{2,1,0:T(2,128)} %all-to-all-done.3.refs_1_.refs_2_), custom_call_target="tpu_custom_call" | custom-call | tf_op jit(solution)/shard_map/cond/branch_1_fun/sweep/pallas_call | solution.py:219
  104.4 17.3 %collective-permute-done.3 = bf16[4,4096]{1,0:T(4,128)(2,1)} collective-permute-done((bf16[4,4096]{1,0:T(4,128)(2,1)S(1)}, bf16[4,4096]{1,0:T(4,128)(2,1)}, u32[]{:S(2)}, u32[]{:S(2)}) %collective-permute-start.3) | collective-permute-done | bytes 32800 | tf_op jit(solution)/shard_map/cond/branch_1_fun/ppermute | solution.py:302
  121.7 2.6 %collective-permute-done.2 = bf16[4,4096]{1,0:T(4,128)(2,1)} collective-permute-done((bf16[4,4096]{1,0:T(4,128)(2,1)S(1)}, bf16[4,4096]{1,0:T(4,128)(2,1)}, u32[]{:S(2)}, u32[]{:S(2)}) %collective-permute-start.2) | collective-permute-done | bytes 32800 | tf_op jit(solution)/shard_map/cond/branch_1_fun/ppermute | solution.py:302
  124.2 16.1 %conditional.5 = (bf16[8,4,4096]{2,1,0:T(4,128)(2,1)S(1)}) conditional(s32[]{:T(128)} %convert_element_type.20, () %tuple.36, (s32[]{:T(128)}, f32[4,4096]{1,0:T(4,128)S(1)}, f32[2,6144]{1,0:T(2,128)S(1)}, f32[8,2,2048]{2,1,0:T(2,128)}, bf16[4,4096]{1,0:T(4,128)(2,1)}, /*index=5*/bf16[4,4096]{1,0:T(4,128)(2,1)}, bf16[4,4096]{1,0:T(4,128)(2,1)}, ...), branch_computations={%region_4.5_spmd, %region_5.6_spmd} | conditional | flops 11 | bytes 524405 | solution.py:280
  124.2 1.9 %block_entries.1 = bf16[8,4,4096]{2,1,0:T(4,128)(2,1)} custom-call(s32[1]{0:T(128)} %bitcast.2.core_ref, f32[4,4096]{1,0:T(4,128)S(1)} %get-tuple-element.78.rate_ref, f32[2,6144]{1,0:T(2,128)S(1)} %get-tuple-element.79.param_ref, f32[8,2,2048]{2,1,0:T(2,128)} %get-tuple-element.80.state_ref, bf16[4,4096]{1,0:T(4,128)(2,1)} %get-tuple-element.81.refs_0_, ...), custom_call_target="tpu_custom_call" | custom-call | tf_op jit(solution)/shard_map/cond/branch_1_fun/block_entries/pallas_call | solution.py:172
  126.1 14.3 %all_to_all.22 = bf16[8,4,4096]{2,1,0:T(4,128)(2,1)S(1)} all-to-all(bf16[8,4,4096]{2,1,0:T(4,128)(2,1)} %block_entries.1), channel_id=1, replica_groups=mesh['plane'=8,'place'=8,'section'=8] {'place'}, dimensions={0} | all-to-all | bytes 524288 | tf_op jit(solution)/shard_map/cond/branch_1_fun/all_to_all | solution.py:269
  141.2 5.2 %finish.1 = bf16[128,4096]{1,0:T(8,128)(2,1)} custom-call(bf16[128,2048]{1,0:T(8,128)(2,1)S(1)} %get-tuple-element.102.refs_0_, bf16[128,2048]{1,0:T(8,128)(2,1)} %copy-done.3, bf16[8,4,4096]{2,1,0:T(4,128)(2,1)S(1)} %get-tuple-element.133.refs_2_, f32[8,2,6144]{2,1,0:T(2,128)} %get-tuple-element.110.refs_3_), custom_call_target="tpu_custom_call" | custom-call | tf_op jit(solution)/shard_map/finish/pallas_call | solution.py:258
  (26 shorter events, 8.9 us)
Async XLA Ops:
  0.0 21.9 %copy-start = (bf16[1,128,4096]{2,1,0:T(8,128)(2,1)S(1)}, bf16[1,128,4096]{2,1,0:T(8,128)(2,1)}, u32[]{:S(2)}) copy-start(bf16[1,128,4096]{2,1,0:T(8,128)(2,1)} %param.11) | copy-start | bytes 3145732
  1.1 20.8 %collective-permute-start.4 = (f32[2,6144]{1,0:T(2,128)S(1)}, f32[2,6144]{1,0:T(2,128)S(1)}, u32[]{:S(2)}, u32[]{:S(2)}) collective-permute-start(f32[2,6144]{1,0:T(2,128)S(1)} %pad_maximum_fusion), channel_id=1, source_target_pairs={{0,263},{1,256},{2,257},{3,258},{4,259},{5,260},{6,261},{7,262},{6... | collective-permute-start | bytes 147464 | tf_op jit(solution)/shard_map/ppermute | solution.py:290
  14.3 7.7 %copy-start.2 = (f32[1,16,4096]{2,1,0:T(8,128)S(1)}, f32[1,16,4096]{2,1,0:T(8,128)}, u32[]{:S(2)}) copy-start(f32[1,16,4096]{2,1,0:T(8,128)} %param.12) | copy-start | bytes 786436
  14.3 7.7 %copy-start.4 = (f32[1,16,4096]{2,1,0:T(8,128)S(1)}, f32[1,16,4096]{2,1,0:T(8,128)}, u32[]{:S(2)}) copy-start(f32[1,16,4096]{2,1,0:T(8,128)} %param.13) | copy-start | bytes 786436
  16.5 58.1 %collective-permute-start.5 = (bf16[128,2048]{1,0:T(8,128)(2,1)}, bf16[128,2048]{1,0:T(8,128)(2,1)S(1)}, u32[]{:S(2)}, u32[]{:S(2)}) collective-permute-start(bf16[128,2048]{1,0:T(8,128)(2,1)} %multiply_convert_fusion), channel_id=1, source_target_pairs={{0,7},{1,0},{2,1},{3,2},{4,3},{5,4},{6,5},{7,6},{8,15},{9,8},{10,9... | collective-permute-start | bytes 1572872 | tf_op jit(solution)/shard_map/ppermute | solution.py:274
  27.5 27.0 %copy-start.1 = (bf16[128,4096]{1,0:T(8,128)(2,1)S(1)}, bf16[128,4096]{1,0:T(8,128)(2,1)}, u32[]{:S(2)}) copy-start(bf16[128,4096]{1,0:T(8,128)(2,1)} %get-tuple-element.68.refs_0_) | copy-start | bytes 3145732 | tf_op jit(solution)/shard_map/cond
  61.3 79.0 %collective-permute-start.6 = (bf16[128,2048]{1,0:T(8,128)(2,1)}, bf16[128,2048]{1,0:T(8,128)(2,1)S(1)}, u32[]{:S(2)}, u32[]{:S(2)}) collective-permute-start(bf16[128,2048]{1,0:T(8,128)(2,1)} %get-tuple-element.103), channel_id=1, source_target_pairs={{0,7},{1,0},{2,1},{3,2},{4,3},{5,4},{6,5},{7,6},{8,15},{9,8},{10,9... | collective-permute-start | bytes 1572872 | tf_op jit(solution)/shard_map/ppermute | solution.py:274
  75.4 14.6 %all-to-all-start.3 = ((f32[8,2,6144]{2,1,0:T(2,128)}), f32[8,2,6144]{2,1,0:T(2,128)}, u32[]{:S(2)}, u32[]{:S(2)}) async-start(f32[8,2,6144]{2,1,0:T(2,128)} %broadcast_in_dim.0), calls=%async_computation.3 | async-start | bytes 786432 | tf_op jit(solution)/shard_map/cond/branch_1_fun/all_to_all | solution.py:269
  81.9 39.8 %collective-permute-start.3 = (bf16[4,4096]{1,0:T(4,128)(2,1)S(1)}, bf16[4,4096]{1,0:T(4,128)(2,1)}, u32[]{:S(2)}, u32[]{:S(2)}) collective-permute-start(bf16[4,4096]{1,0:T(4,128)(2,1)S(1)} %convert_element_type.15), channel_id=1, source_target_pairs={{256,7},{257,0},{258,1},{259,2},{260,3},{261,4},{262,5},{263,6},{3... | collective-permute-start | bytes 98312 | tf_op jit(solution)/shard_map/cond/branch_1_fun/ppermute | solution.py:302
  83.2 41.0 %collective-permute-start.2 = (bf16[4,4096]{1,0:T(4,128)(2,1)S(1)}, bf16[4,4096]{1,0:T(4,128)(2,1)}, u32[]{:S(2)}, u32[]{:S(2)}) collective-permute-start(bf16[4,4096]{1,0:T(4,128)(2,1)S(1)} %convert_element_type.15), channel_id=1, source_target_pairs={{192,7},{193,0},{194,1},{195,2},{196,3},{197,4},{198,5},{199,6},{2... | collective-permute-start | bytes 98312 | tf_op jit(solution)/shard_map/cond/branch_1_fun/ppermute | solution.py:302
  84.5 39.8 %collective-permute-start.1 = (bf16[4,4096]{1,0:T(4,128)(2,1)S(1)}, bf16[4,4096]{1,0:T(4,128)(2,1)}, u32[]{:S(2)}, u32[]{:S(2)}) collective-permute-start(bf16[4,4096]{1,0:T(4,128)(2,1)S(1)} %convert_element_type.15), channel_id=1, source_target_pairs={{128,7},{129,0},{130,1},{131,2},{132,3},{133,4},{134,5},{135,6},{1... | collective-permute-start | bytes 98312 | tf_op jit(solution)/shard_map/cond/branch_1_fun/ppermute | solution.py:302
  86.4 37.8 %collective-permute-start = (bf16[4,4096]{1,0:T(4,128)(2,1)S(1)}, bf16[4,4096]{1,0:T(4,128)(2,1)}, u32[]{:S(2)}, u32[]{:S(2)}) collective-permute-start(bf16[4,4096]{1,0:T(4,128)(2,1)S(1)} %convert_element_type.15), channel_id=1, source_target_pairs={{64,7},{65,0},{66,1},{67,2},{68,3},{69,4},{70,5},{71,6},{128,71},{... | collective-permute-start | bytes 98312 | tf_op jit(solution)/shard_map/cond/branch_1_fun/ppermute | solution.py:302
  93.3 30.9 %all-to-all-start.4 = ((f32[8,2,2048]{2,1,0:T(2,128)}), f32[8,2,2048]{2,1,0:T(2,128)}, u32[]{:S(2)}, u32[]{:S(2)}) async-start(f32[8,2,2048]{2,1,0:T(2,128)} %early_states.1), calls=%async_computation.4 | async-start | bytes 262144 | tf_op jit(solution)/shard_map/cond/branch_1_fun/all_to_all | solution.py:269
  140.3 0.8 copy-start.3

commit v6 on v5

--- a/solution.py
+++ b/solution.py
@@ -233,7 +233,10 @@
     def one_group(group, _):
         lanes = lanes_of(group)
         rates = [mode_row(decay_ref, j, lanes) for j in range(MODES)]
-        leap = [jnp.exp(-8.0 * r) for r in rates]
+        leap = jnp.exp(-8.0 * decay_ref[:, :, lanes])
+        leap = [
+            jnp.broadcast_to(leap[j // SLOT][j % SLOT][None], (8, 128)) for j in range(MODES)
+        ]
         enter = outer_rows(entry_ref, lanes)
         held = [e * jnp.exp(-r * ahead) for e, r in zip(enter, rates)]
         for pair in reversed(range(ROWS // 16)):

time: 148 us -> 148 us (level)
  no operation moved by 1% of the time
where the time goes in v6:
time: 148 us; the launch traced here: 146 us
  starting transfers between devices  43.9 us (30%)
  blocking collectives  39.5 us (27%)
  Pallas kernels  30.6 us (21%)
  waiting for transfers between devices  25.4 us (17%)
  local copies, waits for them, and re-layouts  4.55 us (3%)
  other arithmetic  2.2 us (1%)
    all_to_all x3, blocking collectives, exchange(): return lax.all_to_all(values, axis, split_axis=0, concat_axis=0, tiled=True)  39.5 us
    ppermute x4, waiting for transfers between devices, from_later(): return lax.ppermute(sums, ('plane', 'place', 'section'), pairs)  19.8 us
    ppermute x2, starting transfers between devices, passed_along(): lax.ppermute(shard, axis, [(i, (i + by) % count) for i in range(count)])  14.8 us
    ppermute x1, starting transfers between devices, half_ring(): return lax.ppermute(message, ('plane', 'section'), pairs)  13.1 us
    pallas_call x2, Pallas kernels, sweep(): pl.pallas_call(in_parts(sweep_kernel, len(sources), counts), grid=(channe...  12.9 us
    all_to_all x2, starting transfers between devices, exchange(): return lax.all_to_all(values, axis, split_axis=0, concat_axis=0, tiled=True)  9.53 us
    ppermute x4, starting transfers between devices, from_later(): return lax.ppermute(sums, ('plane', 'place', 'section'), pairs)  6.43 us
    pallas_call x1, Pallas kernels, all_states(): pl.pallas_call(in_parts(state_kernel, 2, [1]), grid=(channels // width,),...  5.59 us
  transfers between devices with their start and end apart: 9, of which 4 were waited for; matrix products, arithmetic and copies ran while one was open for 3% of the time, Pallas kernels for 17%

profile of v6, /device:TPU:64, one launch (start us, length us, event | category | flops | bytes accessed | tf_op | source)
XLA Modules:
  0.0 146.4 jit_solution(16813431249161574086)
XLA Ops:
  1.1 13.1 %collective-permute-start.4 = (f32[2,6144]{1,0:T(2,128)S(1)}, f32[2,6144]{1,0:T(2,128)S(1)}, u32[]{:S(2)}, u32[]{:S(2)}) collective-permute-start(f32[2,6144]{1,0:T(2,128)S(1)} %pad_maximum_fusion), channel_id=1, source_target_pairs={{0,263},{1,256},{2,257},{3,258},{4,259},{5,260},{6,261},{7,262},{6... | collective-permute-start | bytes 147464 | tf_op jit(solution)/shard_map/ppermute | solution.py:293
  14.3 2.2 %multiply_convert_fusion = bf16[128,2048]{1,0:T(8,128)(2,1)} fusion(bf16[128,4096]{1,0:T(8,128)(2,1)} %bitcast.10, bf16[128,4096]{1,0:T(8,128)(2,1)} %bitcast.12), kind=kLoop, calls=%fused_computation.2 | loop fusion | flops 1048576 | bytes 1572864 | tf_op jit(solution)/shard_map/convert_element_type | solution.py:345
  16.5 5.4 %collective-permute-start.5 = (bf16[128,2048]{1,0:T(8,128)(2,1)}, bf16[128,2048]{1,0:T(8,128)(2,1)S(1)}, u32[]{:S(2)}, u32[]{:S(2)}) collective-permute-start(bf16[128,2048]{1,0:T(8,128)(2,1)} %multiply_convert_fusion), channel_id=1, source_target_pairs={{0,7},{1,0},{2,1},{3,2},{4,3},{5,4},{6,5},{7,6},{8,15},{9,8},{10,9... | collective-permute-start | bytes 1572872 | tf_op jit(solution)/shard_map/ppermute | solution.py:277
  21.9 39.4 %conditional.3 = (bf16[128,2048]{1,0:T(8,128)(2,1)}, f32[8,2,6144]{2,1,0:T(2,128)}) conditional(s32[]{:T(128)} %convert_element_type.20, () %tuple.33, (f32[1,16,4096]{2,1,0:T(8,128)S(1)}, bf16[128,4096]{1,0:T(8,128)(2,1)}, bf16[128,4096]{1,0:T(8,128)(2,1)S(1)}, f32[2,4096]{1,0:T(2,128)S(1)}, f32[2,4096]{1,0:T(2,128)S(1)}, ...), branch_computations={%region_0.1_spmd, %region_1.2_spmd} | conditional | bytes 5505068 | solution.py:283
  22.0 5.6 %all_states.1 = f32[8,2,4096]{2,1,0:T(2,128)} custom-call(bf16[128,4096]{1,0:T(8,128)(2,1)} %get-tuple-element.68.refs_0_, bf16[128,4096]{1,0:T(8,128)(2,1)S(1)} %get-tuple-element.69.refs_1_, f32[16,4096]{1,0:T(8,128)S(1)} %bitcast.14), custom_call_target="tpu_custom_call" | custom-call | tf_op jit(solution)/shard_map/cond/branch_1_fun/all_states/pallas_call | solution.py:105
  27.5 12.2 %all_to_all.20.state_ref = f32[8,2,4096]{2,1,0:T(2,128)} all-to-all(f32[8,2,4096]{2,1,0:T(2,128)} %all_states.1), channel_id=1, replica_groups=mesh['plane'=8,'place'=8,'section'=8] {'place'}, dimensions={0} | all-to-all | bytes 524288 | tf_op jit(solution)/shard_map/cond/branch_1_fun/all_to_all | solution.py:272
  39.8 1.7 %plane_sums.1 = f32[8,2,6144]{2,1,0:T(2,128)} custom-call(f32[8,2,4096]{2,1,0:T(2,128)} %all_to_all.20.state_ref, f32[2,4096]{1,0:T(2,128)S(1)} %get-tuple-element.71.rate_ref, f32[2,4096]{1,0:T(2,128)S(1)} %get-tuple-element.72.gain_ref), custom_call_target="tpu_custom_call" | custom-call | tf_op jit(solution)/shard_map/cond/branch_1_fun/plane_sums/pallas_call | solution.py:141
  41.5 13.0 %all_to_all.21.refs_2_ = f32[8,2,6144]{2,1,0:T(2,128)} all-to-all(f32[8,2,6144]{2,1,0:T(2,128)} %plane_sums.1), channel_id=1, replica_groups=mesh['plane'=8,'place'=8,'section'=8] {'place'}, dimensions={0} | all-to-all | bytes 786432 | tf_op jit(solution)/shard_map/cond/branch_1_fun/all_to_all | solution.py:272
  54.6 6.8 %sweep.2 = bf16[128,2048]{1,0:T(8,128)(2,1)} custom-call(bf16[128,4096]{1,0:T(8,128)(2,1)S(1)} %copy-done.1, bf16[128,4096]{1,0:T(8,128)(2,1)S(1)} %get-tuple-element.69.refs_1_, f32[8,2,6144]{2,1,0:T(2,128)} %all_to_all.21.refs_2_, f32[16,4096]{1,0:T(8,128)S(1)} %bitcast.15, f32[16,4096]{1,0:T(8,128)S(1)} %bitcast.16), custom_call_target="tpu_custom_call" | custom-call | tf_op jit(solution)/shard_map/cond/branch_1_fun/sweep/pallas_call | solution.py:219
  61.3 9.4 %collective-permute-start.6 = (bf16[128,2048]{1,0:T(8,128)(2,1)}, bf16[128,2048]{1,0:T(8,128)(2,1)S(1)}, u32[]{:S(2)}, u32[]{:S(2)}) collective-permute-start(bf16[128,2048]{1,0:T(8,128)(2,1)} %get-tuple-element.103), channel_id=1, source_target_pairs={{0,7},{1,0},{2,1},{3,2},{4,3},{5,4},{6,5},{7,6},{8,15},{9,8},{10,9... | collective-permute-start | bytes 1572872 | tf_op jit(solution)/shard_map/ppermute | solution.py:277
  70.7 3.9 %collective-permute-done.5 = bf16[128,2048]{1,0:T(8,128)(2,1)S(1)} collective-permute-done((bf16[128,2048]{1,0:T(8,128)(2,1)}, bf16[128,2048]{1,0:T(8,128)(2,1)S(1)}, u32[]{:S(2)}, u32[]{:S(2)}) %collective-permute-start.5) | collective-permute-done | bytes 524320 | tf_op jit(solution)/shard_map/ppermute | solution.py:277
  74.6 49.6 %conditional.4 = (bf16[128,2048]{1,0:T(8,128)(2,1)S(1)}, f32[8,2,6144]{2,1,0:T(2,128)}, f32[4,4096]{1,0:T(4,128)S(1)}, f32[8,2,2048]{2,1,0:T(2,128)}, bf16[4,409...) conditional(s32[]{:T(128)} %convert_element_type.20, () %tuple.31, ...), branch_computations={%region_2.3_spmd, %region_3.4_spmd} | conditional | flops 22 | bytes 2933260 | solution.py:283
  75.4 5.5 %all-to-all-start.3 = ((f32[8,2,6144]{2,1,0:T(2,128)}), f32[8,2,6144]{2,1,0:T(2,128)}, u32[]{:S(2)}, u32[]{:S(2)}) async-start(f32[8,2,6144]{2,1,0:T(2,128)} %broadcast_in_dim.0), calls=%async_computation.3 | async-start | bytes 786432 | tf_op jit(solution)/shard_map/cond/branch_1_fun/all_to_all | solution.py:272
  84.5 1.9 %collective-permute-start.1 = (bf16[4,4096]{1,0:T(4,128)(2,1)S(1)}, bf16[4,4096]{1,0:T(4,128)(2,1)}, u32[]{:S(2)}, u32[]{:S(2)}) collective-permute-start(bf16[4,4096]{1,0:T(4,128)(2,1)S(1)} %convert_element_type.15), channel_id=1, source_target_pairs={{128,7},{129,0},{130,1},{131,2},{132,3},{133,4},{134,5},{135,6},{1... | collective-permute-start | bytes 98312 | tf_op jit(solution)/shard_map/cond/branch_1_fun/ppermute | solution.py:305
  86.4 1.9 %collective-permute-start = (bf16[4,4096]{1,0:T(4,128)(2,1)S(1)}, bf16[4,4096]{1,0:T(4,128)(2,1)}, u32[]{:S(2)}, u32[]{:S(2)}) collective-permute-start(bf16[4,4096]{1,0:T(4,128)(2,1)S(1)} %convert_element_type.15), channel_id=1, source_target_pairs={{64,7},{65,0},{66,1},{67,2},{68,3},{69,4},{70,5},{71,6},{128,71},{... | collective-permute-start | bytes 98312 | tf_op jit(solution)/shard_map/cond/branch_1_fun/ppermute | solution.py:305
  90.0 3.2 %early_states.1 = f32[8,2,2048]{2,1,0:T(2,128)} custom-call(bf16[128,2048]{1,0:T(8,128)(2,1)S(1)} %get-tuple-element.74.refs_0_, f32[8,2,6144]{2,1,0:T(2,128)} %all-to-all-done.3.refs_1_.refs_2_), custom_call_target="tpu_custom_call" | custom-call | tf_op jit(solution)/shard_map/cond/branch_1_fun/early_states/pallas_call | solution.py:117
  93.3 4.0 %all-to-all-start.4 = ((f32[8,2,2048]{2,1,0:T(2,128)}), f32[8,2,2048]{2,1,0:T(2,128)}, u32[]{:S(2)}, u32[]{:S(2)}) async-start(f32[8,2,2048]{2,1,0:T(2,128)} %early_states.1), calls=%async_computation.4 | async-start | bytes 262144 | tf_op jit(solution)/shard_map/cond/branch_1_fun/all_to_all | solution.py:272
  98.2 6.2 %sweep.3 = bf16[128,2048]{1,0:T(8,128)(2,1)S(1)} custom-call(bf16[128,2048]{1,0:T(8,128)(2,1)S(1)} %get-tuple-element.74.refs_0_, f32[8,2,6144]{2,1,0:T(2,128)} %all-to-all-done.3.refs_1_.refs_2_, f32[8,2,6144]{2,1,0:T(2,128)} %all-to-all-done.3.refs_1_.refs_2_), custom_call_target="tpu_custom_call" | custom-call | tf_op jit(solution)/shard_map/cond/branch_1_fun/sweep/pallas_call | solution.py:219
  104.4 17.3 %collective-permute-done.3 = bf16[4,4096]{1,0:T(4,128)(2,1)} collective-permute-done((bf16[4,4096]{1,0:T(4,128)(2,1)S(1)}, bf16[4,4096]{1,0:T(4,128)(2,1)}, u32[]{:S(2)}, u32[]{:S(2)}) %collective-permute-start.3) | collective-permute-done | bytes 32800 | tf_op jit(solution)/shard_map/cond/branch_1_fun/ppermute | solution.py:305
  121.7 2.6 %collective-permute-done.2 = bf16[4,4096]{1,0:T(4,128)(2,1)} collective-permute-done((bf16[4,4096]{1,0:T(4,128)(2,1)S(1)}, bf16[4,4096]{1,0:T(4,128)(2,1)}, u32[]{:S(2)}, u32[]{:S(2)}) %collective-permute-start.2) | collective-permute-done | bytes 32800 | tf_op jit(solution)/shard_map/cond/branch_1_fun/ppermute | solution.py:305
  124.2 16.1 %conditional.5 = (bf16[8,4,4096]{2,1,0:T(4,128)(2,1)S(1)}) conditional(s32[]{:T(128)} %convert_element_type.20, () %tuple.36, (s32[]{:T(128)}, f32[4,4096]{1,0:T(4,128)S(1)}, f32[2,6144]{1,0:T(2,128)S(1)}, f32[8,2,2048]{2,1,0:T(2,128)}, bf16[4,4096]{1,0:T(4,128)(2,1)}, /*index=5*/bf16[4,4096]{1,0:T(4,128)(2,1)}, bf16[4,4096]{1,0:T(4,128)(2,1)}, ...), branch_computations={%region_4.5_spmd, %region_5.6_spmd} | conditional | flops 11 | bytes 524405 | solution.py:283
  124.2 1.9 %block_entries.1 = bf16[8,4,4096]{2,1,0:T(4,128)(2,1)} custom-call(s32[1]{0:T(128)} %bitcast.2.core_ref, f32[4,4096]{1,0:T(4,128)S(1)} %get-tuple-element.78.rate_ref, f32[2,6144]{1,0:T(2,128)S(1)} %get-tuple-element.79.param_ref, f32[8,2,2048]{2,1,0:T(2,128)} %get-tuple-element.80.state_ref, bf16[4,4096]{1,0:T(4,128)(2,1)} %get-tuple-element.81.refs_0_, ...), custom_call_target="tpu_custom_call" | custom-call | tf_op jit(solution)/shard_map/cond/branch_1_fun/block_entries/pallas_call | solution.py:172
  126.1 14.3 %all_to_all.22 = bf16[8,4,4096]{2,1,0:T(4,128)(2,1)S(1)} all-to-all(bf16[8,4,4096]{2,1,0:T(4,128)(2,1)} %block_entries.1), channel_id=1, replica_groups=mesh['plane'=8,'place'=8,'section'=8] {'place'}, dimensions={0} | all-to-all | bytes 524288 | tf_op jit(solution)/shard_map/cond/branch_1_fun/all_to_all | solution.py:272
  141.2 5.2 %finish.1 = bf16[128,4096]{1,0:T(8,128)(2,1)} custom-call(bf16[128,2048]{1,0:T(8,128)(2,1)S(1)} %get-tuple-element.102.refs_0_, bf16[128,2048]{1,0:T(8,128)(2,1)} %copy-done.3, bf16[8,4,4096]{2,1,0:T(4,128)(2,1)S(1)} %get-tuple-element.133.refs_2_, f32[8,2,6144]{2,1,0:T(2,128)} %get-tuple-element.110.refs_3_), custom_call_target="tpu_custom_call" | custom-call | tf_op jit(solution)/shard_map/finish/pallas_call | solution.py:261
  (26 shorter events, 8.9 us)
Async XLA Ops:
  0.0 21.9 %copy-start = (bf16[1,128,4096]{2,1,0:T(8,128)(2,1)S(1)}, bf16[1,128,4096]{2,1,0:T(8,128)(2,1)}, u32[]{:S(2)}) copy-start(bf16[1,128,4096]{2,1,0:T(8,128)(2,1)} %param.11) | copy-start | bytes 3145732
  1.1 20.8 %collective-permute-start.4 = (f32[2,6144]{1,0:T(2,128)S(1)}, f32[2,6144]{1,0:T(2,128)S(1)}, u32[]{:S(2)}, u32[]{:S(2)}) collective-permute-start(f32[2,6144]{1,0:T(2,128)S(1)} %pad_maximum_fusion), channel_id=1, source_target_pairs={{0,263},{1,256},{2,257},{3,258},{4,259},{5,260},{6,261},{7,262},{6... | collective-permute-start | bytes 147464 | tf_op jit(solution)/shard_map/ppermute | solution.py:293
  14.3 7.7 %copy-start.2 = (f32[1,16,4096]{2,1,0:T(8,128)S(1)}, f32[1,16,4096]{2,1,0:T(8,128)}, u32[]{:S(2)}) copy-start(f32[1,16,4096]{2,1,0:T(8,128)} %param.12) | copy-start | bytes 786436
  14.3 7.7 %copy-start.4 = (f32[1,16,4096]{2,1,0:T(8,128)S(1)}, f32[1,16,4096]{2,1,0:T(8,128)}, u32[]{:S(2)}) copy-start(f32[1,16,4096]{2,1,0:T(8,128)} %param.13) | copy-start | bytes 786436
  16.5 58.1 %collective-permute-start.5 = (bf16[128,2048]{1,0:T(8,128)(2,1)}, bf16[128,2048]{1,0:T(8,128)(2,1)S(1)}, u32[]{:S(2)}, u32[]{:S(2)}) collective-permute-start(bf16[128,2048]{1,0:T(8,128)(2,1)} %multiply_convert_fusion), channel_id=1, source_target_pairs={{0,7},{1,0},{2,1},{3,2},{4,3},{5,4},{6,5},{7,6},{8,15},{9,8},{10,9... | collective-permute-start | bytes 1572872 | tf_op jit(solution)/shard_map/ppermute | solution.py:277
  27.5 27.0 %copy-start.1 = (bf16[128,4096]{1,0:T(8,128)(2,1)S(1)}, bf16[128,4096]{1,0:T(8,128)(2,1)}, u32[]{:S(2)}) copy-start(bf16[128,4096]{1,0:T(8,128)(2,1)} %get-tuple-element.68.refs_0_) | copy-start | bytes 3145732 | tf_op jit(solution)/shard_map/cond
  61.3 79.0 %collective-permute-start.6 = (bf16[128,2048]{1,0:T(8,128)(2,1)}, bf16[128,2048]{1,0:T(8,128)(2,1)S(1)}, u32[]{:S(2)}, u32[]{:S(2)}) collective-permute-start(bf16[128,2048]{1,0:T(8,128)(2,1)} %get-tuple-element.103), channel_id=1, source_target_pairs={{0,7},{1,0},{2,1},{3,2},{4,3},{5,4},{6,5},{7,6},{8,15},{9,8},{10,9... | collective-permute-start | bytes 1572872 | tf_op jit(solution)/shard_map/ppermute | solution.py:277
  75.4 14.6 %all-to-all-start.3 = ((f32[8,2,6144]{2,1,0:T(2,128)}), f32[8,2,6144]{2,1,0:T(2,128)}, u32[]{:S(2)}, u32[]{:S(2)}) async-start(f32[8,2,6144]{2,1,0:T(2,128)} %broadcast_in_dim.0), calls=%async_computation.3 | async-start | bytes 786432 | tf_op jit(solution)/shard_map/cond/branch_1_fun/all_to_all | solution.py:272
  81.9 39.8 %collective-permute-start.3 = (bf16[4,4096]{1,0:T(4,128)(2,1)S(1)}, bf16[4,4096]{1,0:T(4,128)(2,1)}, u32[]{:S(2)}, u32[]{:S(2)}) collective-permute-start(bf16[4,4096]{1,0:T(4,128)(2,1)S(1)} %convert_element_type.15), channel_id=1, source_target_pairs={{256,7},{257,0},{258,1},{259,2},{260,3},{261,4},{262,5},{263,6},{3... | collective-permute-start | bytes 98312 | tf_op jit(solution)/shard_map/cond/branch_1_fun/ppermute | solution.py:305
  83.2 41.0 %collective-permute-start.2 = (bf16[4,4096]{1,0:T(4,128)(2,1)S(1)}, bf16[4,4096]{1,0:T(4,128)(2,1)}, u32[]{:S(2)}, u32[]{:S(2)}) collective-permute-start(bf16[4,4096]{1,0:T(4,128)(2,1)S(1)} %convert_element_type.15), channel_id=1, source_target_pairs={{192,7},{193,0},{194,1},{195,2},{196,3},{197,4},{198,5},{199,6},{2... | collective-permute-start | bytes 98312 | tf_op jit(solution)/shard_map/cond/branch_1_fun/ppermute | solution.py:305
  84.5 39.8 %collective-permute-start.1 = (bf16[4,4096]{1,0:T(4,128)(2,1)S(1)}, bf16[4,4096]{1,0:T(4,128)(2,1)}, u32[]{:S(2)}, u32[]{:S(2)}) collective-permute-start(bf16[4,4096]{1,0:T(4,128)(2,1)S(1)} %convert_element_type.15), channel_id=1, source_target_pairs={{128,7},{129,0},{130,1},{131,2},{132,3},{133,4},{134,5},{135,6},{1... | collective-permute-start | bytes 98312 | tf_op jit(solution)/shard_map/cond/branch_1_fun/ppermute | solution.py:305
  86.4 37.8 %collective-permute-start = (bf16[4,4096]{1,0:T(4,128)(2,1)S(1)}, bf16[4,4096]{1,0:T(4,128)(2,1)}, u32[]{:S(2)}, u32[]{:S(2)}) collective-permute-start(bf16[4,4096]{1,0:T(4,128)(2,1)S(1)} %convert_element_type.15), channel_id=1, source_target_pairs={{64,7},{65,0},{66,1},{67,2},{68,3},{69,4},{70,5},{71,6},{128,71},{... | collective-permute-start | bytes 98312 | tf_op jit(solution)/shard_map/cond/branch_1_fun/ppermute | solution.py:305
  93.3 30.9 %all-to-all-start.4 = ((f32[8,2,2048]{2,1,0:T(2,128)}), f32[8,2,2048]{2,1,0:T(2,128)}, u32[]{:S(2)}, u32[]{:S(2)}) async-start(f32[8,2,2048]{2,1,0:T(2,128)} %early_states.1), calls=%async_computation.4 | async-start | bytes 262144 | tf_op jit(solution)/shard_map/cond/branch_1_fun/all_to_all | solution.py:272
  140.3 0.8 copy-start.3
